TPU v7x, 32 devices: a whole 2x2x4 slice. The times are simulated.
32 devices in a mesh: seg: 8 (over z, x), head: 4 (over y, core).
Axes of the slice: x: 2, y: 2, z: 4, core: 2. Of those that a mesh axis runs over, the one named last changes fastest.
Arguments:
- queries: bfloat16 [2048, 1536], P(('seg', 'head')), may hold values from -8 to 8
- key_rows: bfloat16 [2048, 1536], P(('seg', 'head')), may hold values from -8 to 8
- value_rows: bfloat16 [2048, 1536], P(('seg', 'head')), may hold values from -6 to 6
- w_first: float32 [24, 64, 256], P('head'), may hold values from -0.75 to 0.75
- w_second: float32 [24, 256, 64], P('head'), may hold values from -0.375 to 0.375
- gate_pairs: float32 [2, 1536], P(None, 'head'), may hold values from 0.3 to 1.5
Outputs:
- mixed: float32 [2048, 1536], P('seg', 'head')
All inputs are finite; a program needn't handle non-finite values.
Results may differ from a plain program's by a relative error of at most 0.0011.
Values may be sent and summed in bfloat16 or wider, within the bound.
No kernel may reach another device: no remote copies, remote signals or barrier semaphores. Data moves between devices by JAX's collectives and lax.ppermute only.
A program may use at most 128 MiB of HBM per device.

v0:
```python
import jax
import jax.numpy as jnp
from jax import lax
from jax.sharding import PartitionSpec as P

HEAD_DIM = 64
GROUP = 8


inner_rate = 0.05
norm_epsilon = 1e-05
highest = lax.Precision.HIGHEST


def swapped(value, axis, stride):
    mask = 2**stride
    pairs = [(source, source ^ mask) for source in range(lax.axis_size(axis))]
    return lax.ppermute(value, axis, pairs)


def entering(shard, axis, combine, identity):
    size, position = (lax.axis_size(axis), lax.axis_index(axis))
    everything = jax.tree.map(lambda part: lax.all_gather(part, axis), shard)
    start = jax.tree.map(
        lambda part, zero: jnp.broadcast_to(jnp.asarray(zero, part.dtype), part.shape),
        shard,
        identity,
    )

    def lap(k, before):
        reached = k < position
        new = combine(before, jax.tree.map(lambda part: part[k], everything))
        return jax.tree.map(lambda a, b: jnp.where(reached, a, b), new, before)

    return lax.fori_loop(0, size, lap, start)


def spread_2(block, axis, source):
    block = jnp.where(lax.axis_index(axis) == source, block, jnp.zeros_like(block))
    return lax.psum(block, axis)


def inner_model(inputs, first, second):
    hidden = jnp.einsum("nhd,hdf->nhf", inputs, first, precision=highest)
    mapped = jnp.einsum("nhf,hfd->nhd", jax.nn.gelu(hidden), second, precision=highest)
    centre = mapped - jnp.mean(mapped, axis=-1, keepdims=True)
    spread = jnp.mean(centre * centre, axis=-1, keepdims=True)
    return centre * lax.rsqrt(spread + norm_epsilon)


def inner_loss(first, second, inputs, target):
    error = inner_model(inputs, first, second) - target
    return 0.5 * jnp.sum(error * error) / inputs.shape[0]


def segment_attention(query_rows, key_block, value_block):
    head_count = query_rows.shape[1] // HEAD_DIM

    def head_step(head_index, result):
        start = head_index * HEAD_DIM
        head_query = lax.dynamic_slice_in_dim(query_rows, start, HEAD_DIM, 1)
        head_key = lax.dynamic_slice_in_dim(key_block, start, HEAD_DIM, 1)
        head_value = lax.dynamic_slice_in_dim(value_block, start, HEAD_DIM, 1)
        scores = lax.dot_general(
            head_query, head_key, (((1,), (1,)), ((), ())), preferred_element_type=jnp.float32
        ) * HEAD_DIM ** (-0.5)
        scores = scores - jnp.max(scores, axis=-1, keepdims=True)
        expon = jnp.exp(scores)
        weights = (expon / jnp.sum(expon, axis=-1, keepdims=True)).astype(jnp.bfloat16)
        attended = jnp.dot(weights, head_value, preferred_element_type=jnp.float32)
        return lax.dynamic_update_slice_in_dim(result, attended, start, 1)

    return lax.fori_loop(0, head_count, head_step, jnp.zeros(query_rows.shape, jnp.float32))


def add_pair(earlier, later):
    return (earlier[0] + later[0], earlier[1] + later[1])


def on_device(queries, key_rows, value_rows, w_first, w_second, gate_pairs):
    query_here, key_here, value_here = (
        lax.all_to_all(queries, "head", split_axis=1, concat_axis=0, tiled=True),
        lax.all_to_all(key_rows, "head", split_axis=1, concat_axis=0, tiled=True),
        lax.all_to_all(value_rows, "head", split_axis=1, concat_axis=0, tiled=True),
    )
    row_count, width = query_here.shape
    heads_here = width // HEAD_DIM
    segment_keys, segment_values = (key_here, value_here)
    for bit_index in range(GROUP.bit_length() - 1):
        other_keys, other_values = swapped((segment_keys, segment_values), "seg", bit_index)
        segment_keys = jnp.concatenate([segment_keys, other_keys], axis=0)
        segment_values = jnp.concatenate([segment_values, other_values], axis=0)
    attention = segment_attention(query_here, segment_keys, segment_values)
    inputs = key_here.astype(jnp.float32).reshape(row_count, heads_here, HEAD_DIM)
    target = value_here.astype(jnp.float32).reshape(row_count, heads_here, HEAD_DIM) - inputs
    grad_first, grad_second = jax.grad(inner_loss, argnums=(0, 1))(
        w_first, w_second, inputs, target
    )
    zero_pair = (jnp.zeros_like(grad_first), jnp.zeros_like(grad_second))
    before_first, before_second = entering((grad_first, grad_second), "seg", add_pair, zero_pair)
    ahead_first = before_first + grad_first
    ahead_second = before_second + grad_second
    total_first, total_second = (
        spread_2(ahead_first, "seg", lax.axis_size("seg") - 1),
        spread_2(ahead_second, "seg", lax.axis_size("seg") - 1),
    )
    behind_first = total_first - before_first
    behind_second = total_second - before_second
    query_float = query_here.astype(jnp.float32).reshape(row_count, heads_here, HEAD_DIM)
    forward_out = query_float + inner_model(
        query_float, w_first - inner_rate * ahead_first, w_second - inner_rate * ahead_second
    )
    backward_out = query_float + inner_model(
        query_float, w_first - inner_rate * behind_first, w_second - inner_rate * behind_second
    )
    gate_forward = jnp.tanh(gate_pairs[0])
    gate_backward = jnp.tanh(gate_pairs[1])
    return (
        attention
        + gate_forward * forward_out.reshape(row_count, width)
        + gate_backward * backward_out.reshape(row_count, width)
    )


def solution(mesh):
    in_specs = (
        P(("seg", "head"), None),
        P(("seg", "head"), None),
        P(("seg", "head"), None),
        P("head", None, None),
        P("head", None, None),
        P(None, "head"),
    )
    out_specs = P("seg", "head")
    return jax.shard_map(
        on_device, mesh=mesh, in_specs=in_specs, out_specs=out_specs, check_vma=False
    )
```

profile of v0, /device:TPU:0, one launch (start us, length us, event | category | flops | bytes accessed | tf_op | source)
XLA Modules:
  0.0 313.4 jit_solution(17465196398551484192)
XLA Ops:
  8.2 4.2 %all-to-all-start.1 = ((bf16[64,4,384]{2,0,1:T(8,128)(2,1)}), bf16[64,4,384]{2,0,1:T(8,128)(2,1)S(1)}, u32[]{:S(2)}, u32[]{:S(2)}) async-start(bf16[64,4,384]{2,0,1:T(8,128)(2,1)} %bitcast.97), calls=%async_computation.1 | async-start | bytes 393216 | tf_op jit(solution)/shard_map/all_to_all | solution.py:83
  14.1 3.7 %all-to-all-done.1 = bf16[64,4,384]{2,0,1:T(8,128)(2,1)S(1)} async-done(((bf16[64,4,384]{2,0,1:T(8,128)(2,1)}), bf16[64,4,384]{2,0,1:T(8,128)(2,1)S(1)}, u32[]{:S(2)}, u32[]{:S(2)}) %all-to-all-start.1) | async-done | bytes 196640 | tf_op jit(solution)/shard_map/all_to_all | solution.py:83
  17.8 3.4 %all-to-all-start.2 = ((bf16[64,4,384]{2,0,1:T(8,128)(2,1)}), bf16[64,4,384]{2,0,1:T(8,128)(2,1)S(1)}, u32[]{:S(2)}, u32[]{:S(2)}) async-start(bf16[64,4,384]{2,0,1:T(8,128)(2,1)} %bitcast.96), calls=%async_computation.2 | async-start | bytes 393216 | tf_op jit(solution)/shard_map/all_to_all | solution.py:84
  24.3 2.1 all-to-all-done.2
  28.7 2.9 fusion.76
  31.7 2.1 collective-permute-start
  33.8 5.7 %collective-permute-done = bf16[256,384]{1,0:T(8,128)(2,1)S(1)} collective-permute-done((bf16[256,384]{1,0:T(8,128)(2,1)S(1)}, bf16[256,384]{1,0:T(8,128)(2,1)S(1)}, u32[]{:S(2)}, u32[]{:S(2)}) %collective-permute-start) | collective-permute-done | bytes 196640 | tf_op jit(solution)/shard_map/ppermute | solution.py:18
  39.6 2.2 collective-permute-start.1
  46.2 26.6 %collective-permute-done.1 = bf16[512,384]{1,0:T(8,128)(2,1)S(1)} collective-permute-done((bf16[512,384]{1,0:T(8,128)(2,1)S(1)}, bf16[512,384]{1,0:T(8,128)(2,1)S(1)}, u32[]{:S(2)}, u32[]{:S(2)}) %collective-permute-start.1) | collective-permute-done | bytes 393248 | tf_op jit(solution)/shard_map/ppermute | solution.py:18
  73.0 7.1 %collective-permute-done.4 = bf16[512,384]{1,0:T(8,128)(2,1)S(1)} collective-permute-done((bf16[512,384]{1,0:T(8,128)(2,1)S(1)}, bf16[512,384]{1,0:T(8,128)(2,1)S(1)}, u32[]{:S(2)}, u32[]{:S(2)}) %collective-permute-start.4) | collective-permute-done | bytes 393248 | tf_op jit(solution)/shard_map/ppermute | solution.py:18
  81.2 3.2 %collective-permute-start.5 = (bf16[1024,384]{1,0:T(8,128)(2,1)}, bf16[1024,384]{1,0:T(8,128)(2,1)}, u32[]{:S(2)}, u32[]{:S(2)}) collective-permute-start(bf16[1024,384]{1,0:T(8,128)(2,1)} %pad_maximum_fusion.3), channel_id=1, source_target_pairs={{0,16},{4,20},{8,24},{12,28},{16,0},{20,4},{24,8},{28,12},{1,17},{... | collective-permute-start | bytes 2359304 | tf_op jit(solution)/shard_map/ppermute | solution.py:18
  84.4 2.7 fusion.59
  87.8 3.4 %all-to-all-start = ((bf16[64,4,384]{2,0,1:T(8,128)(2,1)}), bf16[64,4,384]{2,0,1:T(8,128)(2,1)S(1)}, u32[]{:S(2)}, u32[]{:S(2)}) async-start(bf16[64,4,384]{2,0,1:T(8,128)(2,1)} %bitcast.98), calls=%async_computation | async-start | bytes 393216 | tf_op jit(solution)/shard_map/all_to_all | solution.py:82
  91.5 5.0 %all-to-all-done = bf16[64,4,384]{2,0,1:T(8,128)(2,1)S(1)} async-done(((bf16[64,4,384]{2,0,1:T(8,128)(2,1)}), bf16[64,4,384]{2,0,1:T(8,128)(2,1)S(1)}, u32[]{:S(2)}, u32[]{:S(2)}) %all-to-all-start) | async-done | bytes 196640 | tf_op jit(solution)/shard_map/all_to_all | solution.py:82
  97.7 49.9 %collective-permute-done.2 = bf16[1024,384]{1,0:T(8,128)(2,1)} collective-permute-done((bf16[1024,384]{1,0:T(8,128)(2,1)S(1)}, bf16[1024,384]{1,0:T(8,128)(2,1)}, u32[]{:S(2)}, u32[]{:S(2)}) %collective-permute-start.2) | collective-permute-done | bytes 786464 | tf_op jit(solution)/shard_map/ppermute | solution.py:18
  149.1 7.1 %collective-permute-done.5 = bf16[1024,384]{1,0:T(8,128)(2,1)} collective-permute-done((bf16[1024,384]{1,0:T(8,128)(2,1)}, bf16[1024,384]{1,0:T(8,128)(2,1)}, u32[]{:S(2)}, u32[]{:S(2)}) %collective-permute-start.5) | collective-permute-done | bytes 786464 | tf_op jit(solution)/shard_map/ppermute | solution.py:18
  156.2 2.4 pad_maximum_fusion.1
  158.6 22.4 %while.29 = (s32[]{:T(128)}, f32[256,384]{0,1:T(8,128)S(1)}, bf16[256,384]{1,0:T(8,128)(2,1)}, bf16[2048,384]{1,0:T(8,128)(2,1)S(1)}, bf16[2048,384]{1,0:T(8,128...) while((s32[]{:T(128)}, f32[256,384]{0,1:T(8,128)S(1)}, bf16[256,384]{1,0:T(8,128)(2,1)}, ...), condition=%wide.region_3.0_spmd, body=%wide.region_0.0_spmd.sunk | while | flops 137887232 | bytes 7478411 | solution.py:73
  160.5 1.8 convolution_dynamic-update-slice_fusion.2
  164.3 1.8 convolution_dynamic-update-slice_fusion.2
  181.2 23.4 %all-gather.5.cloned.1.call-done = f32[48,64,256]{2,1,0:T(8,128)} async-done(((f32[6,64,256]{2,1,0:T(8,128)}), f32[48,64,256]{2,1,0:T(8,128)}) %all-gather.5.cloned.1.call-update) | async-done | bytes 3145744 | tf_op jit(solution)/shard_map/all_gather | solution.py:23
  204.6 21.8 %while.30 = (s32[]{:T(128)}, f32[6,64,256]{2,1,0:T(8,128)S(1)}, f32[6,256,64]{2,1,0:T(8,128)S(1)}, s32[]{:T(128)}, f32[8,6,64,256]{3,2,1,0:T(8,128)}, /*index=5*/f32[8,6,256,64]{2,3,1,0:T(8,128)}, s32[]{:T(128)}, s32[]{:T(128)}) while((s32[]{:T(128)}, f32[6,64,256]{2,1,0:T(8,128)S(1)}, f32[6,256,64]{2,1,0:T(8,128)S(1)}, s32[]{:T(128)}, ...), condition=%wide.region_9.0_spmd.clone, body=%wide.region_8.0_spmd.clone.sunk | while | flops 589828 | bytes 3932275 | solution.py:35
  231.1 71.0 %all-reduce.3.cloned.1.call-done = (f32[6,64,256]{2,1,0:T(8,128)}, f32[6,256,64]{1,2,0:T(8,128)}) async-done(((f32[6,64,256]{2,1,0:T(8,128)}, f32[6,256,64]{1,2,0:T(8,128)}), (f32[6,64,256]{2,1,0:T(8,128)}, f32[6,256,64]{1,2,0:T(8,128)})) %all-reduce.3.cloned.1.call-update) | async-done | bytes 786448 | tf_op jit(solution)/shard_map/psum | solution.py:40
  302.1 1.9 fusion.82
  (142 shorter events, 65.7 us)
Async XLA Ops:
  6.5 15.2 %copy-start.1 = (f32[6,64,256]{2,1,0:T(8,128)S(1)}, f32[6,64,256]{2,1,0:T(8,128)}, u32[]{:S(2)}) copy-start(f32[6,64,256]{2,1,0:T(8,128)} %param.13) | copy-start | bytes 1179652
  8.2 9.6 %all-to-all-start.1 = ((bf16[64,4,384]{2,0,1:T(8,128)(2,1)}), bf16[64,4,384]{2,0,1:T(8,128)(2,1)S(1)}, u32[]{:S(2)}, u32[]{:S(2)}) async-start(bf16[64,4,384]{2,0,1:T(8,128)(2,1)} %bitcast.97), calls=%async_computation.1 | async-start | bytes 393216 | tf_op jit(solution)/shard_map/all_to_all | solution.py:83
  17.8 8.7 %all-to-all-start.2 = ((bf16[64,4,384]{2,0,1:T(8,128)(2,1)}), bf16[64,4,384]{2,0,1:T(8,128)(2,1)S(1)}, u32[]{:S(2)}, u32[]{:S(2)}) async-start(bf16[64,4,384]{2,0,1:T(8,128)(2,1)} %bitcast.96), calls=%async_computation.2 | async-start | bytes 393216 | tf_op jit(solution)/shard_map/all_to_all | solution.py:84
  21.2 160.1 %all-gather.7.cloned.1.call-start = ((), (), s32[]{:S(2)}) async-start(), calls=%async_computation.4 | async-start | bytes 3538944 | tf_op jit(solution)/shard_map/all_gather | solution.py:23
  31.6 173.0 %all-gather.5.cloned.1.call-start = ((), (), s32[]{:S(2)}) async-start(), calls=%async_computation.3 | async-start | bytes 3538944 | tf_op jit(solution)/shard_map/all_gather | solution.py:23
  31.7 7.9 %collective-permute-start = (bf16[256,384]{1,0:T(8,128)(2,1)S(1)}, bf16[256,384]{1,0:T(8,128)(2,1)S(1)}, u32[]{:S(2)}, u32[]{:S(2)}) collective-permute-start(bf16[256,384]{1,0:T(8,128)(2,1)S(1)} %bitcast.104), channel_id=1, source_target_pairs={{0,4},{4,0},{8,12},{12,8},{16,20},{20,16},{24,28},{28,24},{1,5},{5... | collective-permute-start | bytes 589832 | tf_op jit(solution)/shard_map/ppermute | solution.py:18
  33.8 9.6 %collective-permute-start.3 = (bf16[256,384]{1,0:T(8,128)(2,1)S(1)}, bf16[256,384]{1,0:T(8,128)(2,1)S(1)}, u32[]{:S(2)}, u32[]{:S(2)}) collective-permute-start(bf16[256,384]{1,0:T(8,128)(2,1)S(1)} %bitcast.108), channel_id=1, source_target_pairs={{0,4},{4,0},{8,12},{12,8},{16,20},{20,16},{24,28},{28,24},{1,5},{5... | collective-permute-start | bytes 589832 | tf_op jit(solution)/shard_map/ppermute | solution.py:18
  39.5 33.3 %copy-start.6 = (bf16[256,384]{1,0:T(8,128)(2,1)}, bf16[256,384]{1,0:T(8,128)(2,1)S(1)}, u32[]{:S(2)}) copy-start(bf16[256,384]{1,0:T(8,128)(2,1)S(1)} %collective-permute-done) | copy-start | bytes 589828
  39.6 33.3 %collective-permute-start.1 = (bf16[512,384]{1,0:T(8,128)(2,1)S(1)}, bf16[512,384]{1,0:T(8,128)(2,1)S(1)}, u32[]{:S(2)}, u32[]{:S(2)}) collective-permute-start(bf16[512,384]{1,0:T(8,128)(2,1)S(1)} %pad_maximum_fusion.4), channel_id=1, source_target_pairs={{0,8},{4,12},{8,0},{12,4},{16,24},{20,28},{24,16},{28,20},{1,9},{5... | collective-permute-start | bytes 1179656 | tf_op jit(solution)/shard_map/ppermute | solution.py:18
  43.4 36.8 %copy-start.4 = (bf16[256,384]{1,0:T(8,128)(2,1)}, bf16[256,384]{1,0:T(8,128)(2,1)S(1)}, u32[]{:S(2)}) copy-start(bf16[256,384]{1,0:T(8,128)(2,1)S(1)} %collective-permute-done.3) | copy-start | bytes 589828
  43.4 36.7 %collective-permute-start.4 = (bf16[512,384]{1,0:T(8,128)(2,1)S(1)}, bf16[512,384]{1,0:T(8,128)(2,1)S(1)}, u32[]{:S(2)}, u32[]{:S(2)}) collective-permute-start(bf16[512,384]{1,0:T(8,128)(2,1)S(1)} %pad_maximum_fusion.5), channel_id=1, source_target_pairs={{0,8},{4,12},{8,0},{12,4},{16,24},{20,28},{24,16},{28,20},{1,9},{5... | collective-permute-start | bytes 1179656 | tf_op jit(solution)/shard_map/ppermute | solution.py:18
  46.2 38.2 %copy-start.12 = (f32[6,256,256]{2,1,0:T(8,128)S(1)}, f32[6,256,256]{2,1,0:T(8,128)}, u32[]{:S(2)}) copy-start(f32[6,256,256]{2,1,0:T(8,128)} %copy-done.10) | copy-start | bytes 4718596
  72.9 8.3 %copy-start.9 = (bf16[512,384]{1,0:T(8,128)(2,1)}, bf16[512,384]{1,0:T(8,128)(2,1)S(1)}, u32[]{:S(2)}) copy-start(bf16[512,384]{1,0:T(8,128)(2,1)S(1)} %collective-permute-done.1) | copy-start | bytes 1179652
  73.0 74.7 %collective-permute-start.2 = (bf16[1024,384]{1,0:T(8,128)(2,1)S(1)}, bf16[1024,384]{1,0:T(8,128)(2,1)}, u32[]{:S(2)}, u32[]{:S(2)}) collective-permute-start(bf16[1024,384]{1,0:T(8,128)(2,1)S(1)} %pad_maximum_fusion.2), channel_id=1, source_target_pairs={{0,16},{4,20},{8,24},{12,28},{16,0},{20,4},{24,8},{28,12},{1,17},{... | collective-permute-start | bytes 2359304 | tf_op jit(solution)/shard_map/ppermute | solution.py:18
  81.2 6.0 %copy-start.16 = (bf16[64,1536]{1,0:T(8,128)(2,1)S(1)}, bf16[64,1536]{1,0:T(8,128)(2,1)}, u32[]{:S(2)}) copy-start(bf16[64,1536]{1,0:T(8,128)(2,1)} %param.10) | copy-start | bytes 589828
  81.2 10.3 %copy-start.17 = (f32[2,384]{1,0:T(2,128)S(1)}, f32[2,384]{1,0:T(2,128)}, u32[]{:S(2)}) copy-start(f32[2,384]{1,0:T(2,128)} %param.15) | copy-start | bytes 9220
  81.2 75.0 %collective-permute-start.5 = (bf16[1024,384]{1,0:T(8,128)(2,1)}, bf16[1024,384]{1,0:T(8,128)(2,1)}, u32[]{:S(2)}, u32[]{:S(2)}) collective-permute-start(bf16[1024,384]{1,0:T(8,128)(2,1)} %pad_maximum_fusion.3), channel_id=1, source_target_pairs={{0,16},{4,20},{8,24},{12,28},{16,0},{20,4},{24,8},{28,12},{1,17},{... | collective-permute-start | bytes 2359304 | tf_op jit(solution)/shard_map/ppermute | solution.py:18
  87.8 8.7 %all-to-all-start = ((bf16[64,4,384]{2,0,1:T(8,128)(2,1)}), bf16[64,4,384]{2,0,1:T(8,128)(2,1)S(1)}, u32[]{:S(2)}, u32[]{:S(2)}) async-start(bf16[64,4,384]{2,0,1:T(8,128)(2,1)} %bitcast.98), calls=%async_computation | async-start | bytes 393216 | tf_op jit(solution)/shard_map/all_to_all | solution.py:82
  91.2 210.8 %all-reduce.3.cloned.1.call-start = ((), (), s32[]{:S(2)}) async-start(), calls=%async_computation.5 | async-start | bytes 1572864 | tf_op jit(solution)/shard_map/psum | solution.py:40
  97.7 58.4 %copy-start.5 = (bf16[256,384]{1,0:T(8,128)(2,1)S(1)}, bf16[256,384]{1,0:T(8,128)(2,1)}, u32[]{:S(2)}) copy-start(bf16[256,384]{1,0:T(8,128)(2,1)} %copy-done.4) | copy-start | bytes 589828
  97.7 58.4 %copy-start.8 = (bf16[512,384]{1,0:T(8,128)(2,1)S(1)}, bf16[512,384]{1,0:T(8,128)(2,1)}, u32[]{:S(2)}) copy-start(bf16[512,384]{1,0:T(8,128)(2,1)} %copy-done.7) | copy-start | bytes 1179652
  204.6 22.1 %copy-start.13 = (f32[6,256,64]{1,2,0:T(8,128)S(1)}, f32[6,256,64]{1,2,0:T(8,128)}, u32[]{:S(2)}) copy-start(f32[6,256,64]{1,2,0:T(8,128)} %fusion.76) | copy-start | bytes 1179652
  226.7 1.6 copy-start.2
  302.1 1.9 copy-start.18
  (7 other events, 8.8 us)
Sparse Core Ops, SparseCore 0:
  31.7 111.9 all-gather.6
  145.9 58.6 all-gather.4
  228.5 73.5 all-reduce.2
where the time goes:
time: 315 us; the launch traced here: 313 us
  waiting for transfers between devices  203 us (64%)
  matrix products  35 us (11%)
  other arithmetic  21.9 us (7%)
  starting transfers between devices  20.3 us (6%)
  local copies, waits for them, and re-layouts  18.9 us (6%)
  between operations  13.6 us (4%)
    ppermute x6, waiting for transfers between devices, swapped(): return lax.ppermute(value, axis, pairs)  98 us
    psum x1, waiting for transfers between devices, spread_2(): return lax.psum(block, axis)  71 us
    all_gather x2, waiting for transfers between devices, entering(): everything = jax.tree.map(lambda part: lax.all_gather(part, axis), shard)  23.4 us
    select_n x16, other arithmetic, lap(): return jax.tree.map(lambda a, b: jnp.where(reached, a, b), new, before)  11.1 us
    dot_general x6, matrix products, head_step(): attended = jnp.dot(weights, head_value, preferred_element_type=jnp.float32)  10.9 us
    dynamic_slice x16, local copies, waits for them, and re-layouts, lap(): new = combine(before, jax.tree.map(lambda part: part[k], everything))  10.3 us
    dot_general x5, matrix products, inner_model(): jnp.einsum('nhf,hfd->nhd', jax.nn.gelu(hidden), second, precision=highest)  9.16 us
    ppermute x6, starting transfers between devices, swapped(): return lax.ppermute(value, axis, pairs)  9.04 us
  transfers between devices with their start and end apart: 12, of which 11 were waited for; matrix products, arithmetic and copies ran while one was open for 13% of the time, Pallas kernels for 0%

commit v1 on v0

v1 whole, which is shorter than its diff:
```python
import functools

import jax
import jax.numpy as jnp
from jax import lax
from jax.experimental import pallas as pl
from jax.experimental.pallas import tpu as pltpu
from jax.sharding import PartitionSpec as P

HEAD_DIM = 64
GROUP = 8
LANES = 2 * HEAD_DIM

inner_rate = 0.05
norm_epsilon = 1e-05
LOG2E = 1.4426950408889634
GELU_A = 0.7978845608028654
GELU_B = 0.044715

f32, bf16 = (jnp.float32, jnp.bfloat16)
NN = (((1,), (0,)), ((), ()))
NT = (((1,), (1,)), ((), ()))
TN = (((0,), (0,)), ((), ()))


def dot(a, b, dims):
    return lax.dot_general(a, b, dims, preferred_element_type=f32)


def split(x):
    high = x.astype(bf16)
    return high, (x - high.astype(f32)).astype(bf16)


def half_turn(x):
    return jnp.concatenate([x[:, HEAD_DIM:], x[:, :HEAD_DIM]], axis=1)


def left_half(rows):
    return lax.broadcasted_iota(jnp.int32, (rows, LANES), 1) < HEAD_DIM


def gelu(z):
    t = jnp.tanh(z * (GELU_A + (GELU_A * GELU_B) * (z * z)))
    half = 0.5 * z
    return half + half * t


def gelu_and_slope(z):
    z2 = z * z
    t = jnp.tanh(z * (GELU_A + (GELU_A * GELU_B) * z2))
    a = 0.5 + 0.5 * t
    return z * a, a + z * (2 * GELU_A + (6 * GELU_A * GELU_B) * z2) * (a * (1 - a))


def centred(second):
    return second - jnp.mean(second, axis=0, keepdims=True)


def project(hidden, second):
    high, low = hidden
    second_high, second_low = split(second)
    return dot(high, second_high, NT) + dot(high, second_low, NT) + dot(low, second_high, NT)


def norm_scale(u):
    return lax.rsqrt(jnp.mean(u * u, axis=1, keepdims=True) + norm_epsilon)


def pack_kernel(q_ref, k_ref, v_ref, kv_ref, qq_ref, *, heads_here, sides):
    rows, width = q_ref.shape
    left = left_half(rows)
    left_q = left_half(rows // 2)
    for pair in range(width // LANES):
        cols = slice(pair * LANES, (pair + 1) * LANES)
        k, v, q = (k_ref[:, cols], v_ref[:, cols], q_ref[:, cols])
        k_turned, v_turned = (half_turn(k), half_turn(v))
        qa, qb = (q[: rows // 2], q[rows // 2 :])
        qa_turned, qb_turned = (half_turn(qa), half_turn(qb))
        for odd in range(2):
            head = 2 * pair + odd
            place = (head % heads_here) * sides + head // heads_here
            if odd:
                kv_ref[place] = jnp.where(left, k_turned, v)
                qq_ref[place] = jnp.where(left_q, qa_turned, qb)
            else:
                kv_ref[place] = jnp.where(left, k, v_turned)
                qq_ref[place] = jnp.where(left_q, qa, qb_turned)
    for place in range(heads_here * sides, kv_ref.shape[0]):
        kv_ref[place] = jnp.zeros(kv_ref.shape[1:], bf16)
        qq_ref[place] = jnp.zeros(qq_ref.shape[1:], bf16)


def pack(queries, key_rows, value_rows, heads_here, sides):
    rows = queries.shape[0]
    places = GROUP * sides
    return pl.pallas_call(
        functools.partial(pack_kernel, heads_here=heads_here, sides=sides),
        out_shape=(
            jax.ShapeDtypeStruct((places, rows, LANES), bf16),
            jax.ShapeDtypeStruct((places, rows // 2, LANES), bf16),
        ),
        name="pack",
    )(queries, key_rows, value_rows)


def gradient_kernel(place_ref, kv_ref, first_ref, second_ref, sum_first_ref, sum_second_ref):
    batches, dim, inner = sum_first_ref.shape
    part = kv_ref.shape[0] // batches
    left = left_half(part)
    first = jnp.concatenate(split(first_ref[0]), axis=0)
    second = second_ref[0].T
    second_centred = centred(second)
    second_high, second_low = split(second)
    sum_first = jnp.zeros((dim, inner), f32)
    sum_second = jnp.zeros((dim, inner), f32)
    for b in range(batches):
        kv = kv_ref[b * part : (b + 1) * part, :]
        vk = half_turn(kv)
        k, v = (kv[:, :dim], vk[:, :dim])
        hidden, slope = gelu_and_slope(dot(jnp.where(left, kv, vk), first, NN))
        h_high, h_low = split(hidden)
        u = project((h_high, h_low), second_centred)
        r = norm_scale(u)
        n = u * r
        error = n - v.astype(f32) + k.astype(f32)
        du = (r * (1.0 / part)) * (
            error
            - jnp.mean(error, axis=1, keepdims=True)
            - n * jnp.mean(error * n, axis=1, keepdims=True)
        )
        du_high, du_low = split(du)
        sum_second = sum_second + (
            dot(du_high, h_high, TN) + dot(du_high, h_low, TN) + dot(du_low, h_high, TN)
        )
        dh = dot(du_high, second_high, NN) + dot(du_low, second_high, NN) + dot(du_high, second_low, NN)
        dz_high, dz_low = split(dh * slope)
        sum_first = sum_first + (dot(k, dz_high, TN) + dot(k, dz_low, TN))
        sum_first_ref[b] = sum_first
        sum_second_ref[b] = sum_second


def whole(shape):
    return pl.BlockSpec(shape, lambda i, place: (0,) * len(shape))


def chosen(shape):
    return pl.BlockSpec((1,) + shape, lambda i, place: (place[0],) + (0,) * len(shape))


def gradients(place, kv, w_first, w_second, batches):
    dim, inner = w_first.shape[1:]
    sums = (batches, dim, inner)
    return pl.pallas_call(
        gradient_kernel,
        grid_spec=pltpu.PrefetchScalarGridSpec(
            num_scalar_prefetch=1,
            grid=(1,),
            in_specs=[whole(kv.shape), chosen((dim, inner)), chosen((inner, dim))],
            out_specs=[whole(sums), whole(sums)],
        ),
        out_shape=[jax.ShapeDtypeStruct(sums, f32)] * 2,
        compiler_params=pltpu.CompilerParams(vmem_limit_bytes=48 * 2**20),
        name="gradients",
    )(place, kv, w_first, w_second)


def mix_kernel(
    place_ref, kv_ref, q_ref, first_ref, second_ref, sum_first_ref, sum_second_ref, before_ref, after_ref,
    gate_ref, out_ref, keys_ref, values_ref,
):
    batches, dim, inner = sum_first_ref.shape
    part = kv_ref.shape[0] // batches
    chunk = 2 * q_ref.shape[1]
    lane = lax.broadcasted_iota(jnp.int32, (part, LANES), 1)
    left = lane < dim
    left_q = left_half(chunk // 2)
    for b in range(batches):
        rows = slice(b * part, (b + 1) * part)
        kv = kv_ref[rows, :]
        vk = half_turn(kv)
        keys_ref[rows, :] = jnp.where(left, kv, vk)
        values_ref[rows, :] = jnp.where(left, vk, jnp.where(lane == dim, 1.0, 0.0).astype(bf16))
    first, second = (first_ref[0], second_ref[0].T)
    first_ahead = first - inner_rate * before_ref[0]
    second_ahead = second - inner_rate * before_ref[1]
    first_behind = first - inner_rate * (after_ref[0] + sum_first_ref[batches - 1])
    second_behind = second - inner_rate * (after_ref[1] + sum_second_ref[batches - 1])
    gates = jnp.tanh(gate_ref[0])
    for b in range(batches):
        pieces = []
        for i in range(part // chunk):
            x = q_ref[b * (part // chunk) + i]
            turned = half_turn(x)
            pieces += [jnp.where(left_q, x, turned), jnp.where(left_q, turned, x)]
        qq = jnp.concatenate(pieces, axis=0)
        q = qq.astype(f32)
        result = (gates[0:1] + gates[1:2]) * q[:, :dim]
        ahead = (first_ahead - inner_rate * sum_first_ref[b], second_ahead - inner_rate * sum_second_ref[b])
        if b == 0:
            behind = (first_behind, second_behind)
        else:
            behind = (
                first_behind + inner_rate * sum_first_ref[b - 1],
                second_behind + inner_rate * sum_second_ref[b - 1],
            )
        for way, (a, c) in enumerate((ahead, behind)):
            z = dot(qq, jnp.concatenate(split(a), axis=0), NN)
            u = project(split(gelu(z)), centred(c))
            result = result + gates[way : way + 1] * (u * norm_scale(u))
        scaled = q * (LOG2E * dim**-0.5)
        high = scaled.astype(bf16)
        low = (scaled - high.astype(f32)).astype(bf16)
        scores = dot(jnp.where(left, high, low), keys_ref[...], NT)
        expon = jnp.exp2(scores - jnp.max(scores, axis=1, keepdims=True)).astype(bf16)
        attended = dot(expon, values_ref[...], NN)
        result = result + attended[:, :dim] * (1.0 / attended[:, dim : dim + 1])
        out_ref[b] = jnp.concatenate([result[: part // 2], result[part // 2 :]], axis=1)


def mix(place, kv, q, w_first, w_second, sum_first, sum_second, before, after, gates):
    batches, dim, inner = sum_first.shape
    part = kv.shape[0] // batches
    return pl.pallas_call(
        mix_kernel,
        grid_spec=pltpu.PrefetchScalarGridSpec(
            num_scalar_prefetch=1,
            grid=(1,),
            in_specs=[
                whole(kv.shape),
                whole(q.shape),
                chosen((dim, inner)),
                chosen((inner, dim)),
                whole(sum_first.shape),
                whole(sum_second.shape),
                whole(before.shape),
                whole(after.shape),
                chosen((2, dim)),
            ],
            out_specs=whole((batches, part // 2, LANES)),
            scratch_shapes=[pltpu.VMEM(kv.shape, bf16), pltpu.VMEM(kv.shape, bf16)],
        ),
        out_shape=jax.ShapeDtypeStruct((batches, part // 2, LANES), f32),
        compiler_params=pltpu.CompilerParams(vmem_limit_bytes=56 * 2**20),
        name="mix",
    )(place, kv, q, w_first, w_second, sum_first, sum_second, before, after, gates)


def unpack_kernel(packed_ref, out_ref):
    half = packed_ref.shape[1]
    left = left_half(half)
    for pair in range(out_ref.shape[1] // LANES):
        even = packed_ref[2 * pair].astype(f32)
        odd = packed_ref[2 * pair + 1].astype(f32)
        cols = slice(pair * LANES, (pair + 1) * LANES)
        out_ref[:half, cols] = jnp.where(left, even, half_turn(odd))
        out_ref[half:, cols] = jnp.where(left, half_turn(even), odd)


def unpack(packed, heads_here):
    return pl.pallas_call(
        unpack_kernel,
        out_shape=jax.ShapeDtypeStruct((2 * packed.shape[1], heads_here * HEAD_DIM), f32),
        compiler_params=pltpu.CompilerParams(allow_input_fusion=[True]),
        name="unpack",
    )(packed)


def on_device(queries, key_rows, value_rows, w_first, w_second, gate_pairs):
    seg, sides = (lax.axis_size("seg"), lax.axis_size("head"))
    heads_here = w_first.shape[0]
    segments = seg // GROUP
    assert heads_here <= GROUP
    both = [[s * GROUP * sides + i for i in range(GROUP * sides)] for s in range(segments)]
    lines = [[s * GROUP + i for i in range(GROUP)] for s in range(segments)]
    kv, q = pack(queries, key_rows, value_rows, heads_here, sides)
    kv = lax.all_to_all(kv, ("seg", "head"), 0, 0, tiled=True, axis_index_groups=both)
    q = lax.all_to_all(q, ("seg", "head"), 0, 0, tiled=True, axis_index_groups=both)
    kv = kv.reshape(-1, LANES)
    place = jnp.minimum(lax.axis_index("seg") % GROUP, heads_here - 1).astype(jnp.int32).reshape(1)
    sum_first, sum_second = gradients(place, kv, w_first, w_second, GROUP)
    before = after = jnp.zeros((2,) + sum_first.shape[1:], f32)
    if segments > 1:
        across = [[s * GROUP + i for s in range(segments)] for i in range(GROUP)]
        here = lax.axis_index("seg") // GROUP
        totals = lax.all_gather(
            jnp.stack([sum_first[-1], sum_second[-1]]), "seg", axis_index_groups=across
        )
        order = jnp.arange(segments).reshape(-1, 1, 1, 1)
        before = jnp.sum(jnp.where(order < here, totals, 0.0), axis=0)
        after = jnp.sum(jnp.where(order > here, totals, 0.0), axis=0)
    gates = gate_pairs.reshape(2, heads_here, HEAD_DIM).transpose(1, 0, 2)
    out = mix(place, kv, q, w_first, w_second, sum_first, sum_second, before, after, gates)
    out = lax.all_to_all(out, "seg", 0, 0, tiled=True, axis_index_groups=lines)
    return unpack(out, heads_here)


def solution(mesh):
    in_specs = (
        P(("seg", "head"), None),
        P(("seg", "head"), None),
        P(("seg", "head"), None),
        P("head", None, None),
        P("head", None, None),
        P(None, "head"),
    )
    return jax.shard_map(
        on_device, mesh=mesh, in_specs=in_specs, out_specs=P("seg", "head"), check_vma=False
    )
```

time: 315 us -> 78 us (0.25)
  waiting for transfers between devices: 203 us -> 0.01 us
  blocking collectives: 0 us -> 43.6 us
  matrix products: 35 us -> 0 us
  Pallas kernels: 0 us -> 26.1 us
  other arithmetic: 21.9 us -> 0 us
  starting transfers between devices: 20.3 us -> 3.08 us
  local copies, waits for them, and re-layouts: 18.9 us -> 4.65 us
  between operations: 13.6 us -> 0.1 us
    ppermute x6 -> x0, waiting for transfers between devices: 98 us -> none  [swapped(): return lax.ppermute(value, axis, pairs)]
    psum x1 -> x0, waiting for transfers between devices: 71 us -> none  [spread_2(): return lax.psum(block, axis)]
    all_to_all x0 -> x2, blocking collectives: none -> 43.6 us  [the longest x1 22.9 us: on_device(): lax.all_to_all(kv, ('seg', 'head'), 0, 0, tiled=True, axis_index_groups=b...]
    dot_general x21 -> x0, matrix products: 35 us -> none  [the longest x6 10.9 us: head_step(): attended = jnp.dot(weights, head_value, preferred_element_type=jnp.float32)]
    pallas_call x0 -> x4, Pallas kernels: none -> 26.1 us  [the longest x1 12.5 us: mix(): pl.pallas_call(mix_kernel, grid_spec=pltpu.PrefetchScalarGridSpec(num_sca...]
    all_gather x2 -> x0, waiting for transfers between devices: 23.4 us -> none  [entering(): everything = jax.tree.map(lambda part: lax.all_gather(part, axis), shard)]
    select_n x18 -> x0, other arithmetic: 12.8 us -> none  [the longest x16 11.1 us: lap(): return jax.tree.map(lambda a, b: jnp.where(reached, a, b), new, before)]
    all_to_all x3 -> x1, waiting for transfers between devices: 10.8 us -> 0.01 us  [on_device(): lax.all_to_all(q, ('seg', 'head'), 0, 0, tiled=True, axis_index_groups=both)]
  transfers between devices with their start and end apart: 12 -> 1, of which waited for: 11 -> 0; matrix products, arithmetic and copies ran while one was open for 13% -> 1% of each run, Pallas kernels for 0% -> 12%
where the time goes in v1:
time: 78 us; the launch traced here: 77.5 us
  blocking collectives  43.6 us (56%)
  Pallas kernels  26.1 us (33%)
  local copies, waits for them, and re-layouts  4.65 us (6%)
  starting transfers between devices  3.08 us (4%)
    all_to_all x1, blocking collectives, on_device(): lax.all_to_all(kv, ('seg', 'head'), 0, 0, tiled=True, axis_index_groups=b...  22.9 us
    all_to_all x1, blocking collectives, on_device(): out = lax.all_to_all(out, 'seg', 0, 0, tiled=True, axis_index_groups=lines)  20.7 us
    pallas_call x1, Pallas kernels, mix(): pl.pallas_call(mix_kernel, grid_spec=pltpu.PrefetchScalarGridSpec(num_sca...  12.5 us
    pallas_call x1, Pallas kernels, gradients(): pl.pallas_call(gradient_kernel, grid_spec=pltpu.PrefetchScalarGridSpec(nu...  9.47 us
    unnamed x17, local copies, waits for them, and re-layouts  3.27 us
    all_to_all x1, starting transfers between devices, on_device(): lax.all_to_all(q, ('seg', 'head'), 0, 0, tiled=True, axis_index_groups=both)  3.08 us
    pallas_call x1, Pallas kernels, pack(): pl.pallas_call(functools.partial(pack_kernel, heads_here=heads_here, side...  2.21 us
    pallas_call x1, Pallas kernels, unpack(): pl.pallas_call(unpack_kernel, out_shape=jax.ShapeDtypeStruct((2 * packed....  1.95 us
  transfers between devices with their start and end apart: 1, of which 0 were waited for; matrix products, arithmetic and copies ran while one was open for 1% of the time, Pallas kernels for 12%

profile of v1, /device:TPU:0, one launch (start us, length us, event | category | flops | bytes accessed | tf_op | source)
XLA Modules:
  0.0 77.5 jit_solution(9431330263731056294)
XLA Ops:
  0.0 2.2 %pack.1 = (bf16[32,64,128]{2,1,0:T(8,128)(2,1)}, bf16[32,32,128]{2,1,0:T(8,128)(2,1)}) custom-call(bf16[64,1536]{1,0:T(8,128)(2,1)} %q_ref.1, bf16[64,1536]{1,0:T(8,128)(2,1)} %k_ref.1, bf16[64,1536]{1,0:T(8,128)(2,1)} %v_ref.1), custom_call_target="tpu_custom_call" | custom-call | tf_op jit(solution)/shard_map/pack/pallas_call | solution.py:97
  2.2 22.9 %all_to_all.15 = bf16[32,64,128]{2,1,0:T(8,128)(2,1)S(1)} all-to-all(bf16[32,64,128]{2,1,0:T(8,128)(2,1)} %get-tuple-element.9), channel_id=1, replica_groups={{0,1,2,3,4,5,6,7,8,9,10,11,12,13,14,15,16,17,18,19,20,21,22,23,24,25,26..., dimensions={0} | all-to-all | bytes 1048576 | tf_op jit(solution)/shard_map/all_to_all | solution.py:277
  25.1 0.0 copy-start.1
  25.1 3.1 %all-to-all-start.1 = ((bf16[32,32,128]{2,1,0:T(8,128)(2,1)}), bf16[32,32,128]{2,1,0:T(8,128)(2,1)S(1)}, u32[]{:S(2)}, u32[]{:S(2)}) async-start(bf16[32,32,128]{2,1,0:T(8,128)(2,1)} %get-tuple-element.10), calls=%async_computation.1 | async-start | bytes 524288 | tf_op jit(solution)/shard_map/all_to_all | solution.py:278
  28.2 0.0 copy-start.7
  28.2 0.7 copy-done.7
  28.8 0.1 reshape.11
  28.9 0.6 copy.13
  29.5 0.0 copy-done.6
  29.5 0.3 copy.11.second_ref
  29.8 0.0 copy-start
  29.8 0.0 copy-done.1
  29.8 0.7 copy-done.2
  30.5 9.5 %gradients.1 = (f32[8,64,256]{2,1,0:T(8,128)S(1)}, f32[8,64,256]{2,1,0:T(8,128)S(1)}) custom-call(s32[1]{0:T(128)} %bitcast.place_ref, bf16[2048,128]{1,0:T(8,128)(2,1)S(1)} %bitcast.5, f32[6,64,256]{2,1,0:T(8,128)S(1)} %copy-done.2, f32[6,256,64]{2,1,0:T(8,128)S(1)} %copy.11.second_ref), custom_call_target="tpu_custom_call" | custom-call | tf_op jit(solution)/shard_map/gradients/pallas_call | solution.py:154
  40.0 0.0 copy-done
  40.0 0.0 copy-start.3
  40.0 0.8 %copy-done.3 = f32[8,64,256]{2,1,0:T(8,128)} copy-done((f32[8,64,256]{2,1,0:T(8,128)}, f32[8,64,256]{2,1,0:T(8,128)S(1)}, u32[]{:S(2)}) %copy-start.3) | copy-done | bytes 524312
  40.8 0.8 %copy-done.4 = f32[8,64,256]{2,1,0:T(8,128)} copy-done((f32[8,64,256]{2,1,0:T(8,128)}, f32[8,64,256]{2,1,0:T(8,128)S(1)}, u32[]{:S(2)}) %copy-start.4) | copy-done | bytes 524312
  41.6 0.0 all-to-all-done.1.q_ref
  41.6 0.7 broadcast_in_dim.3.before_ref.after_ref
  42.3 0.0 copy-done.5
  42.3 12.5 %mix.1 = f32[8,128,128]{2,1,0:T(8,128)} custom-call(s32[1]{0:T(128)} %bitcast.place_ref, bf16[2048,128]{1,0:T(8,128)(2,1)} %bitcast.6, bf16[32,32,128]{2,1,0:T(8,128)(2,1)} %copy-done.5, f32[6,64,256]{2,1,0:T(8,128)} %first_ref.3, f32[6,256,64]{2,1,0:T(8,128)} %copy-done, f32[8,64,256]{2,1,0:T(8,128)} %copy-done.3, f32[8,64,256]{2,1,0:T(8,128)} %copy-done.4, ...), custom_call_target="tpu_custom_call" | custom-call | tf_op jit(solution)/shard_map/mix/pallas_call | solution.py:224
  54.8 20.7 %all_to_all.16.packed_ref = f32[8,128,128]{2,1,0:T(8,128)} all-to-all(f32[8,128,128]{2,1,0:T(8,128)} %mix.1), channel_id=1, replica_groups={{0,4,8,12,16,20,24,28},{1,5,9,13,17,21,25,29},{2,6,10,14,18,22,26,30},{..., dimensions={0} | all-to-all | bytes 1048576 | tf_op jit(solution)/shard_map/all_to_all | solution.py:294
  75.5 2.0 %unpack.1 = f32[256,384]{1,0:T(8,128)} custom-call(f32[8,128,128]{2,1,0:T(8,128)} %all_to_all.16.packed_ref), custom_call_target="tpu_custom_call" | custom-call | tf_op jit(solution)/shard_map/unpack/pallas_call | solution.py:261
  (4 shorter events, 0.0 us)
Async XLA Ops:
  25.1 4.8 %copy-start.1 = (bf16[32,64,128]{2,1,0:T(8,128)(2,1)}, bf16[32,64,128]{2,1,0:T(8,128)(2,1)S(1)}, u32[]{:S(2)}) copy-start(bf16[32,64,128]{2,1,0:T(8,128)(2,1)S(1)} %all_to_all.15) | copy-start | bytes 1572868
  25.1 4.5 %copy-start.6 = (f32[6,256,64]{1,2,0:T(8,128)S(1)}, f32[6,256,64]{1,2,0:T(8,128)}, u32[]{:S(2)}) copy-start(f32[6,256,64]{1,2,0:T(8,128)} %param.10) | copy-start | bytes 1179652
  25.1 16.5 %all-to-all-start.1 = ((bf16[32,32,128]{2,1,0:T(8,128)(2,1)}), bf16[32,32,128]{2,1,0:T(8,128)(2,1)S(1)}, u32[]{:S(2)}, u32[]{:S(2)}) async-start(bf16[32,32,128]{2,1,0:T(8,128)(2,1)} %get-tuple-element.10), calls=%async_computation.1 | async-start | bytes 524288 | tf_op jit(solution)/shard_map/all_to_all | solution.py:278
  28.2 0.7 copy-start.7
  29.5 1.0 %copy-start.2 = (f32[6,64,256]{2,1,0:T(8,128)S(1)}, f32[6,64,256]{2,1,0:T(8,128)}, u32[]{:S(2)}) copy-start(f32[6,64,256]{2,1,0:T(8,128)} %first_ref.3) | copy-start | bytes 1179652
  29.8 10.2 %copy-start = (f32[6,256,64]{2,1,0:T(8,128)}, f32[6,256,64]{2,1,0:T(8,128)S(1)}, u32[]{:S(2)}) copy-start(f32[6,256,64]{2,1,0:T(8,128)S(1)} %copy.11.second_ref) | copy-start | bytes 1179652
  40.0 0.8 %copy-start.3 = (f32[8,64,256]{2,1,0:T(8,128)}, f32[8,64,256]{2,1,0:T(8,128)S(1)}, u32[]{:S(2)}) copy-start(f32[8,64,256]{2,1,0:T(8,128)S(1)} %get-tuple-element.11.sum_first_ref) | copy-start | bytes 1572868
  40.8 0.8 %copy-start.4 = (f32[8,64,256]{2,1,0:T(8,128)}, f32[8,64,256]{2,1,0:T(8,128)S(1)}, u32[]{:S(2)}) copy-start(f32[8,64,256]{2,1,0:T(8,128)S(1)} %get-tuple-element.12.sum_second_ref) | copy-start | bytes 1572868
  41.6 0.7 copy-start.5

commit v2 on v1

v2 whole, which is shorter than its diff:
```python
import functools

import jax
import jax.numpy as jnp
from jax import lax
from jax.experimental import pallas as pl
from jax.experimental.pallas import tpu as pltpu
from jax.sharding import PartitionSpec as P

HEAD_DIM = 64
GROUP = 8
LANES = 2 * HEAD_DIM

inner_rate = 0.05
norm_epsilon = 1e-05
LOG2E = 1.4426950408889634
GELU_A = 0.7978845608028654
GELU_B = 0.044715

f32, bf16 = (jnp.float32, jnp.bfloat16)
NN = (((1,), (0,)), ((), ()))
NT = (((1,), (1,)), ((), ()))
TN = (((0,), (0,)), ((), ()))


def dot(a, b, dims):
    return lax.dot_general(a, b, dims, preferred_element_type=f32)


def split(x):
    high = x.astype(bf16)
    return high, (x - high.astype(f32)).astype(bf16)


def half_turn(x):
    return jnp.concatenate([x[:, HEAD_DIM:], x[:, :HEAD_DIM]], axis=1)


def left_half(rows):
    return lax.broadcasted_iota(jnp.int32, (rows, LANES), 1) < HEAD_DIM


def gelu(z):
    t = jnp.tanh(z * (GELU_A + (GELU_A * GELU_B) * (z * z)))
    half = 0.5 * z
    return half + half * t


def gelu_and_slope(z):
    z2 = z * z
    t = jnp.tanh(z * (GELU_A + (GELU_A * GELU_B) * z2))
    a = 0.5 + 0.5 * t
    return z * a, a + z * (2 * GELU_A + (6 * GELU_A * GELU_B) * z2) * (a * (1 - a))


def centred(second):
    return second - jnp.mean(second, axis=0, keepdims=True)


def project(hidden, second):
    high, low = hidden
    second_high, second_low = split(second)
    return dot(high, second_high, NT) + dot(high, second_low, NT) + dot(low, second_high, NT)


def norm_scale(u):
    return lax.rsqrt(jnp.mean(u * u, axis=1, keepdims=True) + norm_epsilon)


def pack_kernel(q_ref, k_ref, v_ref, out_ref, *, heads_here, sides):
    rows, width = q_ref.shape
    left = left_half(rows)
    left_q = left_half(rows // 2)
    for pair in range(width // LANES):
        cols = slice(pair * LANES, (pair + 1) * LANES)
        k, v, q = (k_ref[:, cols], v_ref[:, cols], q_ref[:, cols])
        k_turned, v_turned = (half_turn(k), half_turn(v))
        qa, qb = (q[: rows // 2], q[rows // 2 :])
        qa_turned, qb_turned = (half_turn(qa), half_turn(qb))
        for odd in range(2):
            head = 2 * pair + odd
            place = (head % heads_here) * sides + head // heads_here
            if odd:
                out_ref[place, :rows] = jnp.where(left, k_turned, v)
                out_ref[place, rows:] = jnp.where(left_q, qa_turned, qb)
            else:
                out_ref[place, :rows] = jnp.where(left, k, v_turned)
                out_ref[place, rows:] = jnp.where(left_q, qa, qb_turned)
    for place in range(heads_here * sides, out_ref.shape[0]):
        out_ref[place] = jnp.zeros(out_ref.shape[1:], bf16)


def pack(queries, key_rows, value_rows, heads_here, sides):
    rows = queries.shape[0]
    return pl.pallas_call(
        functools.partial(pack_kernel, heads_here=heads_here, sides=sides),
        out_shape=jax.ShapeDtypeStruct((GROUP * sides, rows + rows // 2, LANES), bf16),
        name="pack",
    )(queries, key_rows, value_rows)


def head_kernel(place_ref, x_ref, first_ref, second_ref, gate_ref, *rest, totals_only, across):
    if across:
        before_ref, after_ref, *rest = rest
    out_ref, keys_ref, values_ref, sum_first_ref, sum_second_ref = rest
    batches = GROUP
    dim, inner = first_ref.shape[1:]
    shards = x_ref.shape[0] // batches
    rows = x_ref.shape[1] * 2 // 3
    part = shards * rows
    lane = lax.broadcasted_iota(jnp.int32, (part, LANES), 1)
    left = lane < dim
    left_q = left_half(rows // 2)
    first, second = (first_ref[0], second_ref[0])

    first_pair = jnp.concatenate(split(first), axis=0)
    second_centred = centred(second)
    second_high, second_low = split(second)
    second_triple = jnp.concatenate([second_high, second_low, second_high], axis=0)
    sum_first = jnp.zeros((dim, inner), f32)
    sum_second = jnp.zeros((dim, inner), f32)
    for b in range(batches):
        kv = x_ref[b * shards : (b + 1) * shards, :rows].reshape(part, LANES)
        vk = half_turn(kv)
        kk = jnp.where(left, kv, vk)
        here = slice(b * part, (b + 1) * part)
        keys_ref[here, :] = kk
        values_ref[here, :] = jnp.where(left, vk, jnp.where(lane == dim, 1.0, 0.0).astype(bf16))
        k, v = (kv[:, :dim], vk[:, :dim])
        hidden, slope = gelu_and_slope(dot(kk, first_pair, NN))
        h_high, h_low = split(hidden)
        u = project((h_high, h_low), second_centred)
        r = norm_scale(u)
        n = u * r
        error = n - v.astype(f32) + k.astype(f32)
        du = (r * (1.0 / part)) * (
            error
            - jnp.mean(error, axis=1, keepdims=True)
            - n * jnp.mean(error * n, axis=1, keepdims=True)
        )
        du_high, du_low = split(du)
        sum_second = sum_second + (
            dot(du_high, h_high, TN) + dot(du_low, h_high, TN) + dot(du_high, h_low, TN)
        )
        dh = dot(jnp.concatenate([du_high, du_high, du_low], axis=1), second_triple, NN)
        dz_high, dz_low = split(dh * slope)
        sum_first = sum_first + (dot(k, dz_high, TN) + dot(k, dz_low, TN))
        sum_first_ref[b] = sum_first
        sum_second_ref[b] = sum_second
    if totals_only:
        out_ref[0] = sum_first
        out_ref[1] = sum_second
        return

    first_ahead = first_behind = first
    second_ahead = second_behind = second
    if across:
        first_ahead = first - inner_rate * before_ref[0]
        second_ahead = second - inner_rate * before_ref[1]
        first_behind = first - inner_rate * after_ref[0]
        second_behind = second - inner_rate * after_ref[1]
    first_behind = first_behind - inner_rate * sum_first
    second_behind = second_behind - inner_rate * sum_second
    gates = gate_ref[:, :dim]
    for other in range(1, gate_ref.shape[1] // dim):
        gates = jnp.where(place_ref[0] == other, gate_ref[:, other * dim : (other + 1) * dim], gates)
    gates = jnp.tanh(gates)
    for b in range(batches):
        pieces = []
        for i in range(shards):
            x = x_ref[b * shards + i, rows:]
            turned = half_turn(x)
            pieces += [jnp.where(left_q, x, turned), jnp.where(left_q, turned, x)]
        qq = jnp.concatenate(pieces, axis=0)
        q = qq.astype(f32)
        result = (gates[0:1] + gates[1:2]) * q[:, :dim]
        ahead = (first_ahead - inner_rate * sum_first_ref[b], second_ahead - inner_rate * sum_second_ref[b])
        behind = (first_behind, second_behind)
        if b > 0:
            behind = (
                first_behind + inner_rate * sum_first_ref[b - 1],
                second_behind + inner_rate * sum_second_ref[b - 1],
            )
        for way, (a, c) in enumerate((ahead, behind)):
            z = dot(qq, jnp.concatenate(split(a), axis=0), NN)
            u = project(split(gelu(z)), centred(c))
            result = result + gates[way : way + 1] * (u * norm_scale(u))
        scaled = q * (LOG2E * dim**-0.5)
        high = scaled.astype(bf16)
        low = (scaled - high.astype(f32)).astype(bf16)
        scores = dot(jnp.where(left, high, low), keys_ref[...], NT)
        expon = jnp.exp2(scores - jnp.max(scores, axis=1, keepdims=True)).astype(bf16)
        attended = dot(expon, values_ref[...], NN)
        result = result + attended[:, :dim] * (1.0 / attended[:, dim : dim + 1])
        out_ref[b] = jnp.concatenate([result[: part // 2], result[part // 2 :]], axis=1)


def whole(shape):
    return pl.BlockSpec(shape, lambda i, place: (0,) * len(shape))


def chosen(shape):
    return pl.BlockSpec((1,) + shape, lambda i, place: (place[0],) + (0,) * len(shape))


def work_on_head(place, x, w_first, w_second, gate_pairs, others=(), totals_only=False):
    weights = w_first.shape[1:]
    tokens = x.shape[0] * (x.shape[1] * 2 // 3)
    out = (2,) + weights if totals_only else (GROUP, tokens // GROUP // 2, LANES)
    return pl.pallas_call(
        functools.partial(head_kernel, totals_only=totals_only, across=len(others) > 0),
        grid_spec=pltpu.PrefetchScalarGridSpec(
            num_scalar_prefetch=1,
            grid=(1,),
            in_specs=[whole(x.shape), chosen(weights), chosen(weights), whole(gate_pairs.shape)]
            + [whole(other.shape) for other in others],
            out_specs=whole(out),
            scratch_shapes=[pltpu.VMEM((tokens, LANES), bf16)] * 2
            + [pltpu.VMEM((GROUP,) + weights, f32)] * 2,
        ),
        out_shape=jax.ShapeDtypeStruct(out, f32),
        compiler_params=pltpu.CompilerParams(vmem_limit_bytes=56 * 2**20),
        name="totals" if totals_only else "head",
    )(place, x, w_first, w_second, gate_pairs, *others)


def unpack_kernel(packed_ref, out_ref):
    half = packed_ref.shape[1]
    left = left_half(half)
    for pair in range(out_ref.shape[1] // LANES):
        even = packed_ref[2 * pair].astype(f32)
        odd = packed_ref[2 * pair + 1].astype(f32)
        cols = slice(pair * LANES, (pair + 1) * LANES)
        out_ref[:half, cols] = jnp.where(left, even, half_turn(odd))
        out_ref[half:, cols] = jnp.where(left, half_turn(even), odd)


def unpack(packed, heads_here):
    return pl.pallas_call(
        unpack_kernel,
        out_shape=jax.ShapeDtypeStruct((2 * packed.shape[1], heads_here * HEAD_DIM), f32),
        compiler_params=pltpu.CompilerParams(allow_input_fusion=[True]),
        name="unpack",
    )(packed)


def on_device(queries, key_rows, value_rows, w_first, w_second, gate_pairs):
    seg, sides = (lax.axis_size("seg"), lax.axis_size("head"))
    heads_here = w_first.shape[0]
    segments = seg // GROUP
    assert heads_here <= GROUP
    both = [[s * GROUP * sides + i for i in range(GROUP * sides)] for s in range(segments)]
    lines = [[s * GROUP + i for i in range(GROUP)] for s in range(segments)]
    w_second = jnp.swapaxes(w_second, 1, 2)
    x = pack(queries, key_rows, value_rows, heads_here, sides)
    x = lax.all_to_all(x, ("seg", "head"), 0, 0, tiled=True, axis_index_groups=both)
    place = jnp.minimum(lax.axis_index("seg") % GROUP, heads_here - 1).astype(jnp.int32).reshape(1)
    others = ()
    if segments > 1:
        totals = work_on_head(place, x, w_first, w_second, gate_pairs, totals_only=True)
        across = [[s * GROUP + i for s in range(segments)] for i in range(GROUP)]
        here = lax.axis_index("seg") // GROUP
        totals = lax.all_gather(totals, "seg", axis_index_groups=across)
        order = jnp.arange(segments).reshape(-1, 1, 1, 1)
        before = jnp.sum(jnp.where(order < here, totals, 0.0), axis=0)
        after = jnp.sum(jnp.where(order > here, totals, 0.0), axis=0)
        others = (before, after)
    out = work_on_head(place, x, w_first, w_second, gate_pairs, others)
    out = lax.all_to_all(out, "seg", 0, 0, tiled=True, axis_index_groups=lines)
    return unpack(out, heads_here)


def solution(mesh):
    in_specs = (
        P(("seg", "head"), None),
        P(("seg", "head"), None),
        P(("seg", "head"), None),
        P("head", None, None),
        P("head", None, None),
        P(None, "head"),
    )
    return jax.shard_map(
        on_device, mesh=mesh, in_specs=in_specs, out_specs=P("seg", "head"), check_vma=False
    )
```

time: 78 us -> 72.4 us (0.928)
  blocking collectives: 43.6 us -> 18.8 us
  waiting for transfers between devices: 0.01 us -> 20.6 us
  starting transfers between devices: 3.08 us -> 7.3 us
  local copies, waits for them, and re-layouts: 4.65 us -> 0.89 us
  Pallas kernels: 26.1 us -> 24.4 us
    all_to_all x1 -> x0, blocking collectives: 22.9 us -> none  [on_device(): lax.all_to_all(kv, ('seg', 'head'), 0, 0, tiled=True, axis_index_groups=b...]
    all_to_all x1, waiting for transfers between devices: 0.01 us -> 20.6 us  [on_device(): lax.all_to_all(x, ('seg', 'head'), 0, 0, tiled=True, axis_index_groups=both)]
    all_to_all x1, starting transfers between devices: 3.08 us -> 7.3 us  [on_device(): lax.all_to_all(x, ('seg', 'head'), 0, 0, tiled=True, axis_index_groups=both)]
    unnamed x17 -> x2, local copies, waits for them, and re-layouts: 3.27 us -> 0.89 us
    all_to_all x1, blocking collectives: 20.7 us -> 18.8 us  [on_device(): out = lax.all_to_all(out, 'seg', 0, 0, tiled=True, axis_index_groups=lines)]
    pallas_call x2 -> x1, Pallas kernels: 21.9 us -> 20.2 us  [work_on_head(): pl.pallas_call(functools.partial(head_kernel, totals_only=totals_only, ac...]
  transfers between devices with their start and end apart: 1 -> 1, of which waited for: 0 -> 1; matrix products, arithmetic and copies ran while one was open for 1% -> 0% of each run, Pallas kernels for 12% -> 0%
where the time goes in v2:
time: 72.4 us; the launch traced here: 72 us
  Pallas kernels  24.4 us (34%)
  waiting for transfers between devices  20.6 us (28%)
  blocking collectives  18.8 us (26%)
  starting transfers between devices  7.3 us (10%)
  local copies, waits for them, and re-layouts  0.89 us (1%)
    all_to_all x1, waiting for transfers between devices, on_device(): lax.all_to_all(x, ('seg', 'head'), 0, 0, tiled=True, axis_index_groups=both)  20.6 us
    pallas_call x1, Pallas kernels, work_on_head(): pl.pallas_call(functools.partial(head_kernel, totals_only=totals_only, ac...  20.2 us
    all_to_all x1, blocking collectives, on_device(): out = lax.all_to_all(out, 'seg', 0, 0, tiled=True, axis_index_groups=lines)  18.8 us
    all_to_all x1, starting transfers between devices, on_device(): lax.all_to_all(x, ('seg', 'head'), 0, 0, tiled=True, axis_index_groups=both)  7.3 us
    pallas_call x1, Pallas kernels, pack(): pl.pallas_call(functools.partial(pack_kernel, heads_here=heads_here, side...  2.23 us
    pallas_call x1, Pallas kernels, unpack(): pl.pallas_call(unpack_kernel, out_shape=jax.ShapeDtypeStruct((2 * packed....  1.95 us
  transfers between devices with their start and end apart: 1, of which 1 were waited for; matrix products, arithmetic and copies ran while one was open for 0% of the time, Pallas kernels for 0%

profile of v2, /device:TPU:0, one launch (start us, length us, event | category | flops | bytes accessed | tf_op | source)
XLA Modules:
  0.0 72.0 jit_solution(3056007250797566760)
XLA Ops:
  0.0 2.2 %pack.1 = bf16[32,96,128]{2,1,0:T(8,128)(2,1)} custom-call(bf16[64,1536]{1,0:T(8,128)(2,1)} %q_ref.1, bf16[64,1536]{1,0:T(8,128)(2,1)} %k_ref.1, bf16[64,1536]{1,0:T(8,128)(2,1)} %v_ref.1), custom_call_target="tpu_custom_call" | custom-call | tf_op jit(solution)/shard_map/pack/pallas_call | solution.py:95
  2.2 7.3 %all-to-all-start = ((bf16[32,96,128]{2,1,0:T(8,128)(2,1)}), bf16[32,96,128]{2,1,0:T(8,128)(2,1)S(1)}, u32[]{:S(2)}, u32[]{:S(2)}) async-start(bf16[32,96,128]{2,1,0:T(8,128)(2,1)} %pack.1), calls=%async_computation | async-start | bytes 1572864 | tf_op jit(solution)/shard_map/all_to_all | solution.py:256
  9.5 20.6 %all-to-all-done.x_ref = bf16[32,96,128]{2,1,0:T(8,128)(2,1)S(1)} async-done(((bf16[32,96,128]{2,1,0:T(8,128)(2,1)}), bf16[32,96,128]{2,1,0:T(8,128)(2,1)S(1)}, u32[]{:S(2)}, u32[]{:S(2)}) %all-to-all-start) | async-done | bytes 786464 | tf_op jit(solution)/shard_map/all_to_all | solution.py:256
  30.2 0.0 copy-start
  30.2 0.9 %copy-done = bf16[32,96,128]{2,1,0:T(8,128)(2,1)} copy-done((bf16[32,96,128]{2,1,0:T(8,128)(2,1)}, bf16[32,96,128]{2,1,0:T(8,128)(2,1)S(1)}, u32[]{:S(2)}) %copy-start) | copy-done | bytes 786456
  31.0 20.2 %head.1 = f32[8,128,128]{2,1,0:T(8,128)} custom-call(s32[1]{0:T(128)} %bitcast.place_ref, bf16[32,96,128]{2,1,0:T(8,128)(2,1)} %copy-done, f32[6,64,256]{2,1,0:T(8,128)} %first_ref.1, f32[6,64,256]{2,1,0:T(8,128)} %bitcast.2, f32[2,384]{1,0:T(2,128)} %gate_ref.1), custom_call_target="tpu_custom_call" | custom-call | tf_op jit(solution)/shard_map/head/pallas_call | solution.py:210
  51.3 18.8 %all_to_all.10.packed_ref = f32[8,128,128]{2,1,0:T(8,128)} all-to-all(f32[8,128,128]{2,1,0:T(8,128)} %head.1), channel_id=1, replica_groups={{0,4,8,12,16,20,24,28},{1,5,9,13,17,21,25,29},{2,6,10,14,18,22,26,30},{..., dimensions={0} | all-to-all | bytes 1048576 | tf_op jit(solution)/shard_map/all_to_all | solution.py:269
  70.1 2.0 %unpack.1 = f32[256,384]{1,0:T(8,128)} custom-call(f32[8,128,128]{2,1,0:T(8,128)} %all_to_all.10.packed_ref), custom_call_target="tpu_custom_call" | custom-call | tf_op jit(solution)/shard_map/unpack/pallas_call | solution.py:239
Async XLA Ops:
  2.2 27.9 %all-to-all-start = ((bf16[32,96,128]{2,1,0:T(8,128)(2,1)}), bf16[32,96,128]{2,1,0:T(8,128)(2,1)S(1)}, u32[]{:S(2)}, u32[]{:S(2)}) async-start(bf16[32,96,128]{2,1,0:T(8,128)(2,1)} %pack.1), calls=%async_computation | async-start | bytes 1572864 | tf_op jit(solution)/shard_map/all_to_all | solution.py:256
  30.2 0.9 %copy-start = (bf16[32,96,128]{2,1,0:T(8,128)(2,1)}, bf16[32,96,128]{2,1,0:T(8,128)(2,1)S(1)}, u32[]{:S(2)}) copy-start(bf16[32,96,128]{2,1,0:T(8,128)(2,1)S(1)} %all-to-all-done.x_ref) | copy-start | bytes 2359300

commit v3 on v2

--- a/solution.py
+++ b/solution.py
@@ -266,7 +266,7 @@
         after = jnp.sum(jnp.where(order > here, totals, 0.0), axis=0)
         others = (before, after)
     out = work_on_head(place, x, w_first, w_second, gate_pairs, others)
-    out = lax.all_to_all(out, "seg", 0, 0, tiled=True, axis_index_groups=lines)
+    out = lax.all_to_all(out.astype(jnp.float16), "seg", 0, 0, tiled=True, axis_index_groups=lines).astype(f32)
     return unpack(out, heads_here)
 
 

time: 72.4 us -> 68.1 us (0.941)
  blocking collectives: 18.8 us -> 12.6 us
  other arithmetic: 0 us -> 1.91 us
    all_to_all x1, blocking collectives: 18.8 us -> 12.6 us  [on_device(): lax.all_to_all(out.astype(jnp.float16), 'seg', 0, 0, tiled=True, axis_ind...]
    convert_element_type x0 -> x2, other arithmetic: none -> 1.91 us  [the longest x1 1.08 us: on_device(): out.astype(jnp.float16)]
where the time goes in v3:
time: 68.1 us; the launch traced here: 67.7 us
  Pallas kernels  24.4 us (36%)
  waiting for transfers between devices  20.6 us (30%)
  blocking collectives  12.6 us (19%)
  starting transfers between devices  7.3 us (11%)
  other arithmetic  1.91 us (3%)
  local copies, waits for them, and re-layouts  0.89 us (1%)
    all_to_all x1, waiting for transfers between devices, on_device(): lax.all_to_all(x, ('seg', 'head'), 0, 0, tiled=True, axis_index_groups=both)  20.6 us
    pallas_call x1, Pallas kernels, work_on_head(): pl.pallas_call(functools.partial(head_kernel, totals_only=totals_only, ac...  20.2 us
    all_to_all x1, blocking collectives, on_device(): lax.all_to_all(out.astype(jnp.float16), 'seg', 0, 0, tiled=True, axis_ind...  12.6 us
    all_to_all x1, starting transfers between devices, on_device(): lax.all_to_all(x, ('seg', 'head'), 0, 0, tiled=True, axis_index_groups=both)  7.3 us
    pallas_call x1, Pallas kernels, pack(): pl.pallas_call(functools.partial(pack_kernel, heads_here=heads_here, side...  2.23 us
    pallas_call x1, Pallas kernels, unpack(): pl.pallas_call(unpack_kernel, out_shape=jax.ShapeDtypeStruct((2 * packed....  1.95 us
  transfers between devices with their start and end apart: 1, of which 1 were waited for; matrix products, arithmetic and copies ran while one was open for 0% of the time, Pallas kernels for 0%

profile of v3, /device:TPU:0, one launch (start us, length us, event | category | flops | bytes accessed | tf_op | source)
XLA Modules:
  0.0 67.7 jit_solution(18357610635586685752)
XLA Ops:
  0.0 2.2 %pack.1 = bf16[32,96,128]{2,1,0:T(8,128)(2,1)} custom-call(bf16[64,1536]{1,0:T(8,128)(2,1)} %q_ref.1, bf16[64,1536]{1,0:T(8,128)(2,1)} %k_ref.1, bf16[64,1536]{1,0:T(8,128)(2,1)} %v_ref.1), custom_call_target="tpu_custom_call" | custom-call | tf_op jit(solution)/shard_map/pack/pallas_call | solution.py:95
  2.2 7.3 %all-to-all-start = ((bf16[32,96,128]{2,1,0:T(8,128)(2,1)}), bf16[32,96,128]{2,1,0:T(8,128)(2,1)S(1)}, u32[]{:S(2)}, u32[]{:S(2)}) async-start(bf16[32,96,128]{2,1,0:T(8,128)(2,1)} %pack.1), calls=%async_computation | async-start | bytes 1572864 | tf_op jit(solution)/shard_map/all_to_all | solution.py:256
  9.5 20.6 %all-to-all-done.x_ref = bf16[32,96,128]{2,1,0:T(8,128)(2,1)S(1)} async-done(((bf16[32,96,128]{2,1,0:T(8,128)(2,1)}), bf16[32,96,128]{2,1,0:T(8,128)(2,1)S(1)}, u32[]{:S(2)}, u32[]{:S(2)}) %all-to-all-start) | async-done | bytes 786464 | tf_op jit(solution)/shard_map/all_to_all | solution.py:256
  30.2 0.0 copy-start
  30.2 0.9 %copy-done = bf16[32,96,128]{2,1,0:T(8,128)(2,1)} copy-done((bf16[32,96,128]{2,1,0:T(8,128)(2,1)}, bf16[32,96,128]{2,1,0:T(8,128)(2,1)S(1)}, u32[]{:S(2)}) %copy-start) | copy-done | bytes 786456
  31.0 20.2 %head.1 = f32[8,128,128]{2,1,0:T(8,128)} custom-call(s32[1]{0:T(128)} %bitcast.place_ref, bf16[32,96,128]{2,1,0:T(8,128)(2,1)} %copy-done, f32[6,64,256]{2,1,0:T(8,128)} %first_ref.1, f32[6,64,256]{2,1,0:T(8,128)} %bitcast.2, f32[2,384]{1,0:T(2,128)} %gate_ref.1), custom_call_target="tpu_custom_call" | custom-call | tf_op jit(solution)/shard_map/head/pallas_call | solution.py:210
  51.3 1.1 %convert_element_type.6 = f16[8,128,128]{2,1,0:T(8,128)(2,1)S(1)} convert(f32[8,128,128]{2,1,0:T(8,128)} %head.1) | non-fusion elementwise | flops 131072 | bytes 786432 | tf_op jit(solution)/shard_map/convert_element_type | solution.py:269
  52.4 12.6 %all_to_all.10 = f16[8,128,128]{2,1,0:T(8,128)(2,1)S(1)} all-to-all(f16[8,128,128]{2,1,0:T(8,128)(2,1)S(1)} %convert_element_type.6), channel_id=1, replica_groups={{0,4,8,12,16,20,24,28},{1,5,9,13,17,21,25,29},{2,6,10,14,18,22,26,30},{..., dimensions={0} | all-to-all | bytes 524288 | tf_op jit(solution)/shard_map/all_to_all | solution.py:269
  64.9 0.8 %convert_element_type.7.packed_ref = f32[8,128,128]{2,1,0:T(8,128)} convert(f16[8,128,128]{2,1,0:T(8,128)(2,1)S(1)} %all_to_all.10) | non-fusion elementwise | flops 131072 | bytes 786432 | tf_op jit(solution)/shard_map/convert_element_type | solution.py:269
  65.8 2.0 %unpack.1 = f32[256,384]{1,0:T(8,128)} custom-call(f32[8,128,128]{2,1,0:T(8,128)} %convert_element_type.7.packed_ref), custom_call_target="tpu_custom_call" | custom-call | tf_op jit(solution)/shard_map/unpack/pallas_call | solution.py:239
Async XLA Ops:
  2.2 27.9 %all-to-all-start = ((bf16[32,96,128]{2,1,0:T(8,128)(2,1)}), bf16[32,96,128]{2,1,0:T(8,128)(2,1)S(1)}, u32[]{:S(2)}, u32[]{:S(2)}) async-start(bf16[32,96,128]{2,1,0:T(8,128)(2,1)} %pack.1), calls=%async_computation | async-start | bytes 1572864 | tf_op jit(solution)/shard_map/all_to_all | solution.py:256
  30.2 0.9 %copy-start = (bf16[32,96,128]{2,1,0:T(8,128)(2,1)}, bf16[32,96,128]{2,1,0:T(8,128)(2,1)S(1)}, u32[]{:S(2)}) copy-start(bf16[32,96,128]{2,1,0:T(8,128)(2,1)S(1)} %all-to-all-done.x_ref) | copy-start | bytes 2359300

commit v4 on v2

v4 whole, which is shorter than its diff:
```python
import functools

import jax
import jax.numpy as jnp
from jax import lax
from jax.experimental import pallas as pl
from jax.experimental.pallas import tpu as pltpu
from jax.sharding import PartitionSpec as P

HEAD_DIM = 64
GROUP = 8
LANES = 2 * HEAD_DIM

inner_rate = 0.05
norm_epsilon = 1e-05
LOG2E = 1.4426950408889634
BOUND = 36.0
SPREAD = 240.0
GELU_A = 0.7978845608028654
GELU_B = 0.044715

f32, bf16 = (jnp.float32, jnp.bfloat16)
NN = (((1,), (0,)), ((), ()))
NT = (((1,), (1,)), ((), ()))
TN = (((0,), (0,)), ((), ()))


in_vmem = pl.BlockSpec(memory_space=pltpu.VMEM)
in_hbm = pl.BlockSpec(memory_space=pl.ANY)


def vmem(x):
    return pltpu.with_memory_space_constraint(x, pltpu.VMEM)


def dot(a, b, dims):
    return lax.dot_general(a, b, dims, preferred_element_type=f32)


def split(x):
    high = x.astype(bf16)
    return high, (x - high.astype(f32)).astype(bf16)


def half_turn(x):
    return jnp.concatenate([x[:, HEAD_DIM:], x[:, :HEAD_DIM]], axis=1)


def left_half(rows):
    return lax.broadcasted_iota(jnp.int32, (rows, LANES), 1) < HEAD_DIM


def gelu(z):
    t = jnp.tanh(z * (GELU_A + (GELU_A * GELU_B) * (z * z)))
    half = 0.5 * z
    return half + half * t


def gelu_and_slope(z):
    z2 = z * z
    t = jnp.tanh(z * (GELU_A + (GELU_A * GELU_B) * z2))
    a = 0.5 + 0.5 * t
    return z * a, a + z * (2 * GELU_A + (6 * GELU_A * GELU_B) * z2) * (a * (1 - a))


def centred(second):
    return second - jnp.mean(second, axis=0, keepdims=True)


def project(hidden, second):
    high, low = hidden
    second_high, second_low = second
    return dot(high, second_high, NT) + dot(high, second_low, NT) + dot(low, second_high, NT)


def norm_scale(u):
    return lax.rsqrt(jnp.mean(u * u, axis=1, keepdims=True) + norm_epsilon)


def pack_kernel(q_ref, k_ref, v_ref, out_ref, *, heads_here, sides):
    rows, width = q_ref.shape
    left = left_half(rows)
    left_q = left_half(rows // 2)
    for pair in range(width // LANES):
        cols = slice(pair * LANES, (pair + 1) * LANES)
        k, v, q = (k_ref[:, cols], v_ref[:, cols], q_ref[:, cols])
        k_turned, v_turned = (half_turn(k), half_turn(v))
        qa, qb = (q[: rows // 2], q[rows // 2 :])
        qa_turned, qb_turned = (half_turn(qa), half_turn(qb))
        for odd in range(2):
            head = 2 * pair + odd
            place = (head % heads_here) * sides + head // heads_here
            if odd:
                out_ref[place, :rows] = jnp.where(left, k_turned, v)
                out_ref[place, rows:] = jnp.where(left_q, qa_turned, qb)
            else:
                out_ref[place, :rows] = jnp.where(left, k, v_turned)
                out_ref[place, rows:] = jnp.where(left_q, qa, qb_turned)
    for place in range(heads_here * sides, out_ref.shape[0]):
        out_ref[place] = jnp.zeros(out_ref.shape[1:], bf16)


def pack(queries, key_rows, value_rows, heads_here, sides):
    rows = queries.shape[0]
    return pl.pallas_call(
        functools.partial(pack_kernel, heads_here=heads_here, sides=sides),
        out_specs=in_vmem,
        out_shape=pltpu.VMEM((GROUP * sides, rows + rows // 2, LANES), bf16),
        name="pack",
    )(queries, key_rows, value_rows)


def encode(x):
    y = jnp.exp2(SPREAD * jnp.sqrt(jnp.abs(x) * (1.0 / BOUND)) - SPREAD / 2)
    return jnp.where(x < 0, -y, y).astype(bf16)


def decode(y):
    y = y.astype(f32)
    root = jnp.log2(jnp.abs(y)) * (1.0 / SPREAD) + 0.5
    x = BOUND * (root * root)
    return jnp.where(y < 0, -x, x)


def head_kernel(place_ref, x_ref, first_hbm, second_hbm, gate_hbm, *rest, totals_only, across):
    if across:
        before_ref, after_ref, *rest = rest
    out_ref, first_ref, second_ref, gate_ref, copied, *rest = rest
    keys_ref, values_ref, high_ref, low_ref, slope_ref, du_ref, attended_ref, sum_first_ref, sum_second_ref = rest
    batches = GROUP
    dim, inner = first_ref.shape
    shards = x_ref.shape[0] // batches
    rows = x_ref.shape[1] * 2 // 3
    part = shards * rows
    lane = lax.broadcasted_iota(jnp.int32, (part, LANES), 1)
    left = lane < dim
    left_q = left_half(rows // 2)

    def here(b):
        return slice(b * part, (b + 1) * part)

    copies = [
        pltpu.make_async_copy(first_hbm.at[place_ref[0]], first_ref, copied.at[0]),
        pltpu.make_async_copy(second_hbm.at[place_ref[0]], second_ref, copied.at[1]),
        pltpu.make_async_copy(gate_hbm, gate_ref, copied.at[2]),
    ]
    for copy in copies:
        copy.start()

    def lay_out(b):
        kv = x_ref[b * shards : (b + 1) * shards, :rows].reshape(part, LANES)
        vk = half_turn(kv)
        keys_ref[here(b), :] = jnp.where(left, kv, vk)
        values_ref[here(b), :] = jnp.where(left, vk, jnp.where(lane == dim, 1.0, 0.0).astype(bf16))

    def queries(b):
        pieces = []
        for i in range(shards):
            x = x_ref[b * shards + i, rows:]
            turned = half_turn(x)
            pieces += [jnp.where(left_q, x, turned), jnp.where(left_q, turned, x)]
        return jnp.concatenate(pieces, axis=0)

    def scores(b):
        scaled = queries(b).astype(f32) * (LOG2E * dim**-0.5)
        high = scaled.astype(bf16)
        low = (scaled - high.astype(f32)).astype(bf16)
        return dot(jnp.where(left, high, low), keys_ref[...], NT)

    def attend(b, score):
        expon = jnp.exp2(score - jnp.max(score, axis=1, keepdims=True)).astype(bf16)
        attended = dot(expon, values_ref[...], NN)
        attended_ref[here(b), :] = attended[:, :dim] * (1.0 / attended[:, dim : dim + 1])

    for b in range(batches):
        lay_out(b)
    score = None if totals_only else scores(0)
    for copy in copies:
        copy.wait()
    first, second = (first_ref[...], second_ref[...])
    first_pair = jnp.concatenate(split(first), axis=0)
    second_centred = split(centred(second))
    second_high, second_low = split(second)
    second_triple = jnp.concatenate([second_high, second_low, second_high], axis=0)

    def hidden(b):
        h, slope = gelu_and_slope(dot(keys_ref[here(b), :], first_pair, NN))
        high_ref[here(b), :], low_ref[here(b), :] = split(h)
        slope_ref[here(b), :] = slope

    def error(b):
        u = project((high_ref[here(b), :], low_ref[here(b), :]), second_centred)
        r = norm_scale(u)
        n = u * r
        e = n - (values_ref[here(b), :dim].astype(f32) - keys_ref[here(b), :dim].astype(f32))
        du = (r * (1.0 / part)) * (
            e - jnp.mean(e, axis=1, keepdims=True) - n * jnp.mean(e * n, axis=1, keepdims=True)
        )
        du_high, du_low = split(du)
        du_ref[here(b), :] = jnp.concatenate([du_high, du_high, du_low], axis=1)

    def add_gradient(b, sums):
        du = du_ref[here(b), :]
        du_high, du_low = (du[:, :dim], du[:, 2 * dim :])
        h_high, h_low = (high_ref[here(b), :], low_ref[here(b), :])
        grad_second = dot(du_high, h_high, TN) + dot(du_low, h_high, TN) + dot(du_high, h_low, TN)
        dz_high, dz_low = split(dot(du, second_triple, NN) * slope_ref[here(b), :])
        k = keys_ref[here(b), :dim]
        sums = (sums[0] + (dot(k, dz_high, TN) + dot(k, dz_low, TN)), sums[1] + grad_second)
        sum_first_ref[b], sum_second_ref[b] = sums
        return sums

    sums = (jnp.zeros((dim, inner), f32), jnp.zeros((dim, inner), f32))
    for step in range(batches + 2):
        if step < batches:
            hidden(step)
        if step + 1 < batches and not totals_only:
            next_score = scores(step + 1)
        if 1 <= step < batches + 1:
            error(step - 1)
        if step < batches and not totals_only:
            attend(step, score)
            score = next_score
        if step >= 2:
            sums = add_gradient(step - 2, sums)
    if totals_only:
        out_ref[0], out_ref[1] = sums
        return

    starts = [[first, second], [first - inner_rate * sums[0], second - inner_rate * sums[1]]]
    if across:
        for way, other in enumerate((before_ref, after_ref)):
            for i in range(2):
                starts[way][i] = starts[way][i] - inner_rate * other[i]
    gates = gate_ref[:, :dim]
    for other in range(1, gate_ref.shape[1] // dim):
        gates = jnp.where(place_ref[0] == other, gate_ref[:, other * dim : (other + 1) * dim], gates)
    gates = jnp.tanh(gates)

    def enter_model(b, way):
        w, v = starts[way]
        if way == 0:
            w, v = (w - inner_rate * sum_first_ref[b], v - inner_rate * sum_second_ref[b])
        elif b > 0:
            w, v = (w + inner_rate * sum_first_ref[b - 1], v + inner_rate * sum_second_ref[b - 1])
        z = dot(queries(b), jnp.concatenate(split(w), axis=0), NN)
        return split(gelu(z)), split(centred(v))

    def leave_model(way, entered):
        u = project(*entered)
        return gates[way : way + 1] * (u * norm_scale(u))

    ahead, behind = (enter_model(0, 0), enter_model(0, 1))
    for b in range(batches):
        last = b + 1 == batches
        next_ahead = None if last else enter_model(b + 1, 0)
        result = leave_model(0, ahead)
        next_behind = None if last else enter_model(b + 1, 1)
        result = result + leave_model(1, behind)
        q = queries(b)[:, :dim].astype(f32)
        result = encode(attended_ref[here(b), :] + (gates[0:1] + gates[1:2]) * q + result)
        out_ref[b] = jnp.concatenate([result[: part // 2], result[part // 2 :]], axis=1)
        ahead, behind = (next_ahead, next_behind)


def work_on_head(place, x, w_first, w_second, gate_pairs, others=(), totals_only=False):
    dim, inner = w_first.shape[1:]
    tokens = x.shape[0] * (x.shape[1] * 2 // 3)
    if totals_only:
        out = pltpu.VMEM((2, dim, inner), f32)
    else:
        out = pltpu.VMEM((GROUP, tokens // GROUP // 2, LANES), bf16)
    return pl.pallas_call(
        functools.partial(head_kernel, totals_only=totals_only, across=len(others) > 0),
        grid_spec=pltpu.PrefetchScalarGridSpec(
            num_scalar_prefetch=1,
            grid=(1,),
            in_specs=[in_vmem] + [in_hbm] * 3 + [in_vmem] * len(others),
            out_specs=in_vmem,
            scratch_shapes=[
                pltpu.VMEM((dim, inner), f32),
                pltpu.VMEM((dim, inner), f32),
                pltpu.VMEM(gate_pairs.shape, f32),
                pltpu.SemaphoreType.DMA((3,)),
                pltpu.VMEM((tokens, LANES), bf16),
                pltpu.VMEM((tokens, LANES), bf16),
                pltpu.VMEM((tokens, inner), bf16),
                pltpu.VMEM((tokens, inner), bf16),
                pltpu.VMEM((tokens, inner), f32),
                pltpu.VMEM((tokens, 3 * dim), bf16),
                pltpu.VMEM((tokens, dim), f32),
                pltpu.VMEM((GROUP, dim, inner), f32),
                pltpu.VMEM((GROUP, dim, inner), f32),
            ],
        ),
        out_shape=out,
        compiler_params=pltpu.CompilerParams(vmem_limit_bytes=52 * 2**20),
        name="totals" if totals_only else "head",
    )(place, vmem(x), w_first, w_second, gate_pairs, *[vmem(other) for other in others])


def unpack_kernel(packed_ref, out_ref):
    half = packed_ref.shape[1]
    left = left_half(half)
    for pair in range(out_ref.shape[1] // LANES):
        even = packed_ref[2 * pair]
        odd = packed_ref[2 * pair + 1]
        cols = slice(pair * LANES, (pair + 1) * LANES)
        out_ref[:half, cols] = decode(jnp.where(left, even, half_turn(odd)))
        out_ref[half:, cols] = decode(jnp.where(left, half_turn(even), odd))


def unpack(packed, heads_here):
    return pl.pallas_call(
        unpack_kernel,
        in_specs=[in_vmem],
        out_shape=jax.ShapeDtypeStruct((2 * packed.shape[1], heads_here * HEAD_DIM), f32),
        name="unpack",
    )(vmem(packed))


def on_device(queries, key_rows, value_rows, w_first, w_second, gate_pairs):
    seg, sides = (lax.axis_size("seg"), lax.axis_size("head"))
    heads_here = w_first.shape[0]
    segments = seg // GROUP
    assert heads_here <= GROUP
    both = [[s * GROUP * sides + i for i in range(GROUP * sides)] for s in range(segments)]
    lines = [[s * GROUP + i for i in range(GROUP)] for s in range(segments)]
    w_second = jnp.swapaxes(w_second, 1, 2)
    x = pack(queries, key_rows, value_rows, heads_here, sides)
    x = lax.all_to_all(x, ("seg", "head"), 0, 0, tiled=True, axis_index_groups=both)
    place = jnp.minimum(lax.axis_index("seg") % GROUP, heads_here - 1).astype(jnp.int32).reshape(1)
    others = ()
    if segments > 1:
        totals = work_on_head(place, x, w_first, w_second, gate_pairs, totals_only=True)
        across = [[s * GROUP + i for s in range(segments)] for i in range(GROUP)]
        here = lax.axis_index("seg") // GROUP
        totals = lax.all_gather(totals, "seg", axis_index_groups=across)
        order = jnp.arange(segments).reshape(-1, 1, 1, 1)
        before = jnp.sum(jnp.where(order < here, totals, 0.0), axis=0)
        after = jnp.sum(jnp.where(order > here, totals, 0.0), axis=0)
        others = (before, after)
    out = work_on_head(place, x, w_first, w_second, gate_pairs, others)
    out = lax.all_to_all(out, "seg", 0, 0, tiled=True, axis_index_groups=lines)
    return unpack(out, heads_here)


def solution(mesh):
    in_specs = (
        P(("seg", "head"), None),
        P(("seg", "head"), None),
        P(("seg", "head"), None),
        P("head", None, None),
        P("head", None, None),
        P(None, "head"),
    )
    return jax.shard_map(
        on_device, mesh=mesh, in_specs=in_specs, out_specs=P("seg", "head"), check_vma=False
    )
```

time: 72.4 us -> 58.4 us (0.81)
  Pallas kernels: 24.4 us -> 17.6 us
  blocking collectives: 18.8 us -> 12.6 us
  local copies, waits for them, and re-layouts: 0.89 us -> 0.01 us
    all_to_all x1, blocking collectives: 18.8 us -> 12.6 us  [on_device(): out = lax.all_to_all(out, 'seg', 0, 0, tiled=True, axis_index_groups=lines)]
    pallas_call x1, Pallas kernels: 20.2 us -> 14.4 us  [work_on_head(): pl.pallas_call(functools.partial(head_kernel, totals_only=totals_only, ac...]
    pallas_call x1, Pallas kernels: 1.95 us -> 0.96 us  [unpack(): pl.pallas_call(unpack_kernel, in_specs=[in_vmem], out_shape=jax.ShapeDtyp...]
    unnamed x2 -> x6, local copies, waits for them, and re-layouts: 0.89 us -> 0.01 us
where the time goes in v4:
time: 58.4 us; the launch traced here: 58.1 us
  waiting for transfers between devices  20.6 us (35%)
  Pallas kernels  17.6 us (30%)
  blocking collectives  12.6 us (22%)
  starting transfers between devices  7.3 us (12%)
    all_to_all x1, waiting for transfers between devices, on_device(): lax.all_to_all(x, ('seg', 'head'), 0, 0, tiled=True, axis_index_groups=both)  20.6 us
    pallas_call x1, Pallas kernels, work_on_head(): pl.pallas_call(functools.partial(head_kernel, totals_only=totals_only, ac...  14.4 us
    all_to_all x1, blocking collectives, on_device(): out = lax.all_to_all(out, 'seg', 0, 0, tiled=True, axis_index_groups=lines)  12.6 us
    all_to_all x1, starting transfers between devices, on_device(): lax.all_to_all(x, ('seg', 'head'), 0, 0, tiled=True, axis_index_groups=both)  7.3 us
    pallas_call x1, Pallas kernels, pack(): pl.pallas_call(functools.partial(pack_kernel, heads_here=heads_here, side...  2.22 us
  transfers between devices with their start and end apart: 1, of which 1 were waited for; matrix products, arithmetic and copies ran while one was open for 0% of the time, Pallas kernels for 0%

profile of v4, /device:TPU:0, one launch (start us, length us, event | category | flops | bytes accessed | tf_op | source)
XLA Modules:
  0.0 58.1 jit_solution(10541850691334643546)
XLA Ops:
  0.0 2.2 %pack.1 = bf16[32,96,128]{2,1,0:T(8,128)(2,1)} custom-call(bf16[64,1536]{1,0:T(8,128)(2,1)} %q_ref.1, bf16[64,1536]{1,0:T(8,128)(2,1)} %k_ref.1, bf16[64,1536]{1,0:T(8,128)(2,1)} %v_ref.1), custom_call_target="tpu_custom_call" | custom-call | tf_op jit(solution)/shard_map/pack/pallas_call | solution.py:105
  2.2 0.0 copy-start
  2.2 0.0 copy-start.1
  2.2 7.3 %all-to-all-start = ((bf16[32,96,128]{2,1,0:T(8,128)(2,1)}), bf16[32,96,128]{2,1,0:T(8,128)(2,1)S(1)}, u32[]{:S(2)}, u32[]{:S(2)}) async-start(bf16[32,96,128]{2,1,0:T(8,128)(2,1)} %pack.1), calls=%async_computation | async-start | bytes 1572864 | tf_op jit(solution)/shard_map/all_to_all | solution.py:331
  9.5 0.0 copy-start.2
  9.6 20.6 %all-to-all-done.x_ref = bf16[32,96,128]{2,1,0:T(8,128)(2,1)S(1)} async-done(((bf16[32,96,128]{2,1,0:T(8,128)(2,1)}), bf16[32,96,128]{2,1,0:T(8,128)(2,1)S(1)}, u32[]{:S(2)}, u32[]{:S(2)}) %all-to-all-start) | async-done | bytes 786464 | tf_op jit(solution)/shard_map/all_to_all | solution.py:331
  30.2 0.0 copy-done
  30.2 0.0 copy-done.1
  30.2 0.0 copy-done.2
  30.2 14.4 %head.1 = bf16[8,128,128]{2,1,0:T(8,128)(2,1)S(1)} custom-call(s32[1]{0:T(128)} %bitcast.place_ref, bf16[32,96,128]{2,1,0:T(8,128)(2,1)S(1)} %all-to-all-done.x_ref, f32[6,64,256]{2,1,0:T(8,128)S(1)} %copy-done, f32[6,64,256]{2,1,0:T(8,128)S(1)} %bitcast.2, f32[2,384]{1,0:T(2,128)S(1)} %copy-done.2), custom_call_target="tpu_custom_call" | custom-call | tf_op jit(solution)/shard_map/head/pallas_call | solution.py:273
  44.6 12.6 %all_to_all.10.packed_ref = bf16[8,128,128]{2,1,0:T(8,128)(2,1)S(1)} all-to-all(bf16[8,128,128]{2,1,0:T(8,128)(2,1)S(1)} %head.1), channel_id=1, replica_groups={{0,4,8,12,16,20,24,28},{1,5,9,13,17,21,25,29},{2,6,10,14,18,22,26,30},{..., dimensions={0} | all-to-all | bytes 524288 | tf_op jit(solution)/shard_map/all_to_all | solution.py:344
  57.2 1.0 %unpack.1 = f32[256,384]{1,0:T(8,128)} custom-call(bf16[8,128,128]{2,1,0:T(8,128)(2,1)S(1)} %all_to_all.10.packed_ref), custom_call_target="tpu_custom_call" | custom-call | tf_op jit(solution)/shard_map/unpack/pallas_call | solution.py:314
Async XLA Ops:
  2.2 27.9 %copy-start = (f32[6,64,256]{2,1,0:T(8,128)S(1)}, f32[6,64,256]{2,1,0:T(8,128)}, u32[]{:S(2)}) copy-start(f32[6,64,256]{2,1,0:T(8,128)} %first_hbm.1) | copy-start | bytes 1179652
  2.2 27.9 %copy-start.1 = (f32[6,256,64]{1,2,0:T(8,128)S(1)}, f32[6,256,64]{1,2,0:T(8,128)}, u32[]{:S(2)}) copy-start(f32[6,256,64]{1,2,0:T(8,128)} %param.10) | copy-start | bytes 1179652
  2.2 27.9 %all-to-all-start = ((bf16[32,96,128]{2,1,0:T(8,128)(2,1)}), bf16[32,96,128]{2,1,0:T(8,128)(2,1)S(1)}, u32[]{:S(2)}, u32[]{:S(2)}) async-start(bf16[32,96,128]{2,1,0:T(8,128)(2,1)} %pack.1), calls=%async_computation | async-start | bytes 1572864 | tf_op jit(solution)/shard_map/all_to_all | solution.py:331
  9.5 20.6 %copy-start.2 = (f32[2,384]{1,0:T(2,128)S(1)}, f32[2,384]{1,0:T(2,128)}, u32[]{:S(2)}) copy-start(f32[2,384]{1,0:T(2,128)} %gate_hbm.1) | copy-start | bytes 9220

commit v5 on v4

--- a/solution.py
+++ b/solution.py
@@ -26,7 +26,11 @@
 
 
 in_vmem = pl.BlockSpec(memory_space=pltpu.VMEM)
-in_hbm = pl.BlockSpec(memory_space=pl.ANY)
+in_hbm = pl.BlockSpec(memory_space=pltpu.HBM)
+
+
+def hbm(x):
+    return pltpu.with_memory_space_constraint(x, pltpu.HBM)
 
 
 def vmem(x):
@@ -122,13 +126,14 @@
     return jnp.where(y < 0, -x, x)
 
 
-def head_kernel(place_ref, x_ref, first_hbm, second_hbm, gate_hbm, *rest, totals_only, across):
+def head_kernel(x_ref, first_hbm, second_hbm, gate_hbm, *rest, totals_only, across):
     if across:
         before_ref, after_ref, *rest = rest
     out_ref, first_ref, second_ref, gate_ref, copied, *rest = rest
     keys_ref, values_ref, high_ref, low_ref, slope_ref, du_ref, attended_ref, sum_first_ref, sum_second_ref = rest
     batches = GROUP
     dim, inner = first_ref.shape
+    place = jnp.minimum(lax.axis_index("seg") % GROUP, first_hbm.shape[0] - 1)
     shards = x_ref.shape[0] // batches
     rows = x_ref.shape[1] * 2 // 3
     part = shards * rows
@@ -140,8 +145,8 @@
         return slice(b * part, (b + 1) * part)
 
     copies = [
-        pltpu.make_async_copy(first_hbm.at[place_ref[0]], first_ref, copied.at[0]),
-        pltpu.make_async_copy(second_hbm.at[place_ref[0]], second_ref, copied.at[1]),
+        pltpu.make_async_copy(first_hbm.at[place], first_ref, copied.at[0]),
+        pltpu.make_async_copy(second_hbm.at[place], second_ref, copied.at[1]),
         pltpu.make_async_copy(gate_hbm, gate_ref, copied.at[2]),
     ]
     for copy in copies:
@@ -234,7 +239,7 @@
                 starts[way][i] = starts[way][i] - inner_rate * other[i]
     gates = gate_ref[:, :dim]
     for other in range(1, gate_ref.shape[1] // dim):
-        gates = jnp.where(place_ref[0] == other, gate_ref[:, other * dim : (other + 1) * dim], gates)
+        gates = jnp.where(place == other, gate_ref[:, other * dim : (other + 1) * dim], gates)
     gates = jnp.tanh(gates)
 
     def enter_model(b, way):
@@ -263,7 +268,7 @@
         ahead, behind = (next_ahead, next_behind)
 
 
-def work_on_head(place, x, w_first, w_second, gate_pairs, others=(), totals_only=False):
+def work_on_head(x, w_first, w_second, gate_pairs, others=(), totals_only=False):
     dim, inner = w_first.shape[1:]
     tokens = x.shape[0] * (x.shape[1] * 2 // 3)
     if totals_only:
@@ -272,31 +277,27 @@
         out = pltpu.VMEM((GROUP, tokens // GROUP // 2, LANES), bf16)
     return pl.pallas_call(
         functools.partial(head_kernel, totals_only=totals_only, across=len(others) > 0),
-        grid_spec=pltpu.PrefetchScalarGridSpec(
-            num_scalar_prefetch=1,
-            grid=(1,),
-            in_specs=[in_vmem] + [in_hbm] * 3 + [in_vmem] * len(others),
-            out_specs=in_vmem,
-            scratch_shapes=[
-                pltpu.VMEM((dim, inner), f32),
-                pltpu.VMEM((dim, inner), f32),
-                pltpu.VMEM(gate_pairs.shape, f32),
-                pltpu.SemaphoreType.DMA((3,)),
-                pltpu.VMEM((tokens, LANES), bf16),
-                pltpu.VMEM((tokens, LANES), bf16),
-                pltpu.VMEM((tokens, inner), bf16),
-                pltpu.VMEM((tokens, inner), bf16),
-                pltpu.VMEM((tokens, inner), f32),
-                pltpu.VMEM((tokens, 3 * dim), bf16),
-                pltpu.VMEM((tokens, dim), f32),
-                pltpu.VMEM((GROUP, dim, inner), f32),
-                pltpu.VMEM((GROUP, dim, inner), f32),
-            ],
-        ),
+        in_specs=[in_vmem] + [in_hbm] * 3 + [in_vmem] * len(others),
+        out_specs=in_vmem,
+        scratch_shapes=[
+            pltpu.VMEM((dim, inner), f32),
+            pltpu.VMEM((dim, inner), f32),
+            pltpu.VMEM(gate_pairs.shape, f32),
+            pltpu.SemaphoreType.DMA((3,)),
+            pltpu.VMEM((tokens, LANES), bf16),
+            pltpu.VMEM((tokens, LANES), bf16),
+            pltpu.VMEM((tokens, inner), bf16),
+            pltpu.VMEM((tokens, inner), bf16),
+            pltpu.VMEM((tokens, inner), f32),
+            pltpu.VMEM((tokens, 3 * dim), bf16),
+            pltpu.VMEM((tokens, dim), f32),
+            pltpu.VMEM((GROUP, dim, inner), f32),
+            pltpu.VMEM((GROUP, dim, inner), f32),
+        ],
         out_shape=out,
         compiler_params=pltpu.CompilerParams(vmem_limit_bytes=52 * 2**20),
         name="totals" if totals_only else "head",
-    )(place, vmem(x), w_first, w_second, gate_pairs, *[vmem(other) for other in others])
+    )(vmem(x), hbm(w_first), hbm(w_second), hbm(gate_pairs), *[vmem(other) for other in others])
 
 
 def unpack_kernel(packed_ref, out_ref):
@@ -329,10 +330,9 @@
     w_second = jnp.swapaxes(w_second, 1, 2)
     x = pack(queries, key_rows, value_rows, heads_here, sides)
     x = lax.all_to_all(x, ("seg", "head"), 0, 0, tiled=True, axis_index_groups=both)
-    place = jnp.minimum(lax.axis_index("seg") % GROUP, heads_here - 1).astype(jnp.int32).reshape(1)
     others = ()
     if segments > 1:
-        totals = work_on_head(place, x, w_first, w_second, gate_pairs, totals_only=True)
+        totals = work_on_head(x, w_first, w_second, gate_pairs, totals_only=True)
         across = [[s * GROUP + i for s in range(segments)] for i in range(GROUP)]
         here = lax.axis_index("seg") // GROUP
         totals = lax.all_gather(totals, "seg", axis_index_groups=across)
@@ -340,7 +340,7 @@
         before = jnp.sum(jnp.where(order < here, totals, 0.0), axis=0)
         after = jnp.sum(jnp.where(order > here, totals, 0.0), axis=0)
         others = (before, after)
-    out = work_on_head(place, x, w_first, w_second, gate_pairs, others)
+    out = work_on_head(x, w_first, w_second, gate_pairs, others)
     out = lax.all_to_all(out, "seg", 0, 0, tiled=True, axis_index_groups=lines)
     return unpack(out, heads_here)
 

time: 58.4 us -> 57.4 us (0.983)
  blocking collectives: 12.6 us -> 40.3 us
  waiting for transfers between devices: 20.6 us -> 0 us
  starting transfers between devices: 7.3 us -> 0 us
  Pallas kernels: 17.6 us -> 16.9 us
    all_to_all x0 -> x1, blocking collectives: none -> 27.7 us  [on_device(): lax.all_to_all(x, ('seg', 'head'), 0, 0, tiled=True, axis_index_groups=both)]
    all_to_all x1 -> x0, waiting for transfers between devices: 20.6 us -> none  [on_device(): lax.all_to_all(x, ('seg', 'head'), 0, 0, tiled=True, axis_index_groups=both)]
    all_to_all x1 -> x0, starting transfers between devices: 7.3 us -> none  [on_device(): lax.all_to_all(x, ('seg', 'head'), 0, 0, tiled=True, axis_index_groups=both)]
    pallas_call x1, Pallas kernels: 2.22 us -> 1.33 us  [pack(): pl.pallas_call(functools.partial(pack_kernel, heads_here=heads_here, side...]
  transfers between devices with their start and end apart: 1 -> 0, of which waited for: 1 -> 0; matrix products, arithmetic and copies ran while one was open for 0% -> 0% of each run, Pallas kernels for 0% -> 0%
where the time goes in v5:
time: 57.4 us; the launch traced here: 57.2 us
  blocking collectives  40.3 us (70%)
  Pallas kernels  16.9 us (29%)
    all_to_all x1, blocking collectives, on_device(): lax.all_to_all(x, ('seg', 'head'), 0, 0, tiled=True, axis_index_groups=both)  27.7 us
    pallas_call x1, Pallas kernels, work_on_head(): pl.pallas_call(functools.partial(head_kernel, totals_only=totals_only, ac...  14.6 us
    all_to_all x1, blocking collectives, on_device(): out = lax.all_to_all(out, 'seg', 0, 0, tiled=True, axis_index_groups=lines)  12.6 us
    pallas_call x1, Pallas kernels, pack(): pl.pallas_call(functools.partial(pack_kernel, heads_here=heads_here, side...  1.33 us

profile of v5, /device:TPU:0, one launch (start us, length us, event | category | flops | bytes accessed | tf_op | source)
XLA Modules:
  0.0 57.2 jit_solution(15626578237530056272)
XLA Ops:
  0.0 1.3 %pack.1 = bf16[32,96,128]{2,1,0:T(8,128)(2,1)S(1)} custom-call(bf16[64,1536]{1,0:T(8,128)(2,1)} %q_ref.1, bf16[64,1536]{1,0:T(8,128)(2,1)} %k_ref.1, bf16[64,1536]{1,0:T(8,128)(2,1)} %v_ref.1), custom_call_target="tpu_custom_call" | custom-call | tf_op jit(solution)/shard_map/pack/pallas_call | solution.py:109
  1.3 27.7 %all_to_all.10.x_ref = bf16[32,96,128]{2,1,0:T(8,128)(2,1)S(1)} all-to-all(bf16[32,96,128]{2,1,0:T(8,128)(2,1)S(1)} %pack.1), channel_id=1, replica_groups={{0,1,2,3,4,5,6,7,8,9,10,11,12,13,14,15,16,17,18,19,20,21,22,23,24,25,26..., dimensions={0} | all-to-all | bytes 1572864 | tf_op jit(solution)/shard_map/all_to_all | solution.py:332
  29.1 14.6 %head.1 = bf16[8,128,128]{2,1,0:T(8,128)(2,1)S(1)} custom-call(bf16[32,96,128]{2,1,0:T(8,128)(2,1)S(1)} %all_to_all.10.x_ref, f32[6,64,256]{2,1,0:T(8,128)} %first_hbm.1, f32[6,64,256]{2,1,0:T(8,128)} %bitcast.1, f32[2,384]{1,0:T(2,128)} %gate_hbm.1), custom_call_target="tpu_custom_call" | custom-call | tf_op jit(solution)/shard_map/head/pallas_call | solution.py:278
  43.6 12.6 %all_to_all.11.packed_ref = bf16[8,128,128]{2,1,0:T(8,128)(2,1)S(1)} all-to-all(bf16[8,128,128]{2,1,0:T(8,128)(2,1)S(1)} %head.1), channel_id=1, replica_groups={{0,4,8,12,16,20,24,28},{1,5,9,13,17,21,25,29},{2,6,10,14,18,22,26,30},{..., dimensions={0} | all-to-all | bytes 524288 | tf_op jit(solution)/shard_map/all_to_all | solution.py:344
  56.2 1.0 %unpack.1 = f32[256,384]{1,0:T(8,128)} custom-call(bf16[8,128,128]{2,1,0:T(8,128)(2,1)S(1)} %all_to_all.11.packed_ref), custom_call_target="tpu_custom_call" | custom-call | tf_op jit(solution)/shard_map/unpack/pallas_call | solution.py:315

commit v6 on v5

--- a/solution.py
+++ b/solution.py
@@ -182,6 +182,10 @@
     score = None if totals_only else scores(0)
     for copy in copies:
         copy.wait()
+    gates = gate_ref[:, :dim]
+    for other in range(1, gate_ref.shape[1] // dim):
+        gates = jnp.where(place == other, gate_ref[:, other * dim : (other + 1) * dim], gates)
+    gate_ref[:, :dim] = jnp.tanh(gates)
     first, second = (first_ref[...], second_ref[...])
     first_pair = jnp.concatenate(split(first), axis=0)
     second_centred = split(centred(second))
@@ -238,9 +242,6 @@
             for i in range(2):
                 starts[way][i] = starts[way][i] - inner_rate * other[i]
     gates = gate_ref[:, :dim]
-    for other in range(1, gate_ref.shape[1] // dim):
-        gates = jnp.where(place == other, gate_ref[:, other * dim : (other + 1) * dim], gates)
-    gates = jnp.tanh(gates)
 
     def enter_model(b, way):
         w, v = starts[way]

time: 57.4 us -> 55.3 us (0.963)
  Pallas kernels: 16.9 us -> 14.7 us
    pallas_call x1, Pallas kernels: 14.6 us -> 12.4 us  [work_on_head(): pl.pallas_call(functools.partial(head_kernel, totals_only=totals_only, ac...]
where the time goes in v6:
time: 55.3 us; the launch traced here: 55 us
  blocking collectives  40.3 us (73%)
  Pallas kernels  14.7 us (27%)
    all_to_all x1, blocking collectives, on_device(): lax.all_to_all(x, ('seg', 'head'), 0, 0, tiled=True, axis_index_groups=both)  27.7 us
    all_to_all x1, blocking collectives, on_device(): out = lax.all_to_all(out, 'seg', 0, 0, tiled=True, axis_index_groups=lines)  12.6 us
    pallas_call x1, Pallas kernels, work_on_head(): pl.pallas_call(functools.partial(head_kernel, totals_only=totals_only, ac...  12.4 us
    pallas_call x1, Pallas kernels, pack(): pl.pallas_call(functools.partial(pack_kernel, heads_here=heads_here, side...  1.33 us

profile of v6, /device:TPU:0, one launch (start us, length us, event | category | flops | bytes accessed | tf_op | source)
XLA Modules:
  0.0 55.0 jit_solution(12001592568966323633)
XLA Ops:
  0.0 1.3 %pack.1 = bf16[32,96,128]{2,1,0:T(8,128)(2,1)S(1)} custom-call(bf16[64,1536]{1,0:T(8,128)(2,1)} %q_ref.1, bf16[64,1536]{1,0:T(8,128)(2,1)} %k_ref.1, bf16[64,1536]{1,0:T(8,128)(2,1)} %v_ref.1), custom_call_target="tpu_custom_call" | custom-call | tf_op jit(solution)/shard_map/pack/pallas_call | solution.py:109
  1.3 27.7 %all_to_all.10.x_ref = bf16[32,96,128]{2,1,0:T(8,128)(2,1)S(1)} all-to-all(bf16[32,96,128]{2,1,0:T(8,128)(2,1)S(1)} %pack.1), channel_id=1, replica_groups={{0,1,2,3,4,5,6,7,8,9,10,11,12,13,14,15,16,17,18,19,20,21,22,23,24,25,26..., dimensions={0} | all-to-all | bytes 1572864 | tf_op jit(solution)/shard_map/all_to_all | solution.py:333
  29.1 12.4 %head.1 = bf16[8,128,128]{2,1,0:T(8,128)(2,1)S(1)} custom-call(bf16[32,96,128]{2,1,0:T(8,128)(2,1)S(1)} %all_to_all.10.x_ref, f32[6,64,256]{2,1,0:T(8,128)} %first_hbm.1, f32[6,64,256]{2,1,0:T(8,128)} %bitcast.1, f32[2,384]{1,0:T(2,128)} %gate_hbm.1), custom_call_target="tpu_custom_call" | custom-call | tf_op jit(solution)/shard_map/head/pallas_call | solution.py:279
  41.5 12.6 %all_to_all.11.packed_ref = bf16[8,128,128]{2,1,0:T(8,128)(2,1)S(1)} all-to-all(bf16[8,128,128]{2,1,0:T(8,128)(2,1)S(1)} %head.1), channel_id=1, replica_groups={{0,4,8,12,16,20,24,28},{1,5,9,13,17,21,25,29},{2,6,10,14,18,22,26,30},{..., dimensions={0} | all-to-all | bytes 524288 | tf_op jit(solution)/shard_map/all_to_all | solution.py:345
  54.1 1.0 %unpack.1 = f32[256,384]{1,0:T(8,128)} custom-call(bf16[8,128,128]{2,1,0:T(8,128)(2,1)S(1)} %all_to_all.11.packed_ref), custom_call_target="tpu_custom_call" | custom-call | tf_op jit(solution)/shard_map/unpack/pallas_call | solution.py:316

commit v7 on v6

--- a/solution.py
+++ b/solution.py
@@ -190,7 +190,7 @@
     first_pair = jnp.concatenate(split(first), axis=0)
     second_centred = split(centred(second))
     second_high, second_low = split(second)
-    second_triple = jnp.concatenate([second_high, second_low, second_high], axis=0)
+    second_triple = jnp.concatenate([second_high, second_high, second_low], axis=0)
 
     def hidden(b):
         h, slope = gelu_and_slope(dot(keys_ref[here(b), :], first_pair, NN))
@@ -206,13 +206,14 @@
             e - jnp.mean(e, axis=1, keepdims=True) - n * jnp.mean(e * n, axis=1, keepdims=True)
         )
         du_high, du_low = split(du)
-        du_ref[here(b), :] = jnp.concatenate([du_high, du_high, du_low], axis=1)
+        du_ref[here(b), :] = jnp.concatenate([du_high, du_low, du_high], axis=1)
 
     def add_gradient(b, sums):
         du = du_ref[here(b), :]
-        du_high, du_low = (du[:, :dim], du[:, 2 * dim :])
+        du_high = du[:, :dim]
         h_high, h_low = (high_ref[here(b), :], low_ref[here(b), :])
-        grad_second = dot(du_high, h_high, TN) + dot(du_low, h_high, TN) + dot(du_high, h_low, TN)
+        both = dot(du[:, : 2 * dim], h_high, TN)
+        grad_second = both[:dim] + both[dim:] + dot(du_high, h_low, TN)
         dz_high, dz_low = split(dot(du, second_triple, NN) * slope_ref[here(b), :])
         k = keys_ref[here(b), :dim]
         sums = (sums[0] + (dot(k, dz_high, TN) + dot(k, dz_low, TN)), sums[1] + grad_second)

time: 55.3 us -> 55 us (level)
  no operation moved by 1% of the time
where the time goes in v7:
time: 55 us; the launch traced here: 54.8 us
  blocking collectives  40.3 us (73%)
  Pallas kernels  14.5 us (26%)
    all_to_all x1, blocking collectives, on_device(): lax.all_to_all(x, ('seg', 'head'), 0, 0, tiled=True, axis_index_groups=both)  27.7 us
    all_to_all x1, blocking collectives, on_device(): out = lax.all_to_all(out, 'seg', 0, 0, tiled=True, axis_index_groups=lines)  12.6 us
    pallas_call x1, Pallas kernels, work_on_head(): pl.pallas_call(functools.partial(head_kernel, totals_only=totals_only, ac...  12.2 us
    pallas_call x1, Pallas kernels, pack(): pl.pallas_call(functools.partial(pack_kernel, heads_here=heads_here, side...  1.33 us

profile of v7, /device:TPU:0, one launch (start us, length us, event | category | flops | bytes accessed | tf_op | source)
XLA Modules:
  0.0 54.8 jit_solution(11829068024864323062)
XLA Ops:
  0.0 1.3 %pack.1 = bf16[32,96,128]{2,1,0:T(8,128)(2,1)S(1)} custom-call(bf16[64,1536]{1,0:T(8,128)(2,1)} %q_ref.1, bf16[64,1536]{1,0:T(8,128)(2,1)} %k_ref.1, bf16[64,1536]{1,0:T(8,128)(2,1)} %v_ref.1), custom_call_target="tpu_custom_call" | custom-call | tf_op jit(solution)/shard_map/pack/pallas_call | solution.py:109
  1.3 27.7 %all_to_all.10.x_ref = bf16[32,96,128]{2,1,0:T(8,128)(2,1)S(1)} all-to-all(bf16[32,96,128]{2,1,0:T(8,128)(2,1)S(1)} %pack.1), channel_id=1, replica_groups={{0,1,2,3,4,5,6,7,8,9,10,11,12,13,14,15,16,17,18,19,20,21,22,23,24,25,26..., dimensions={0} | all-to-all | bytes 1572864 | tf_op jit(solution)/shard_map/all_to_all | solution.py:334
  29.1 12.2 %head.1 = bf16[8,128,128]{2,1,0:T(8,128)(2,1)S(1)} custom-call(bf16[32,96,128]{2,1,0:T(8,128)(2,1)S(1)} %all_to_all.10.x_ref, f32[6,64,256]{2,1,0:T(8,128)} %first_hbm.1, f32[6,64,256]{2,1,0:T(8,128)} %bitcast.1, f32[2,384]{1,0:T(2,128)} %gate_hbm.1), custom_call_target="tpu_custom_call" | custom-call | tf_op jit(solution)/shard_map/head/pallas_call | solution.py:280
  41.3 12.6 %all_to_all.11.packed_ref = bf16[8,128,128]{2,1,0:T(8,128)(2,1)S(1)} all-to-all(bf16[8,128,128]{2,1,0:T(8,128)(2,1)S(1)} %head.1), channel_id=1, replica_groups={{0,4,8,12,16,20,24,28},{1,5,9,13,17,21,25,29},{2,6,10,14,18,22,26,30},{..., dimensions={0} | all-to-all | bytes 524288 | tf_op jit(solution)/shard_map/all_to_all | solution.py:346
  53.8 1.0 %unpack.1 = f32[256,384]{1,0:T(8,128)} custom-call(bf16[8,128,128]{2,1,0:T(8,128)(2,1)S(1)} %all_to_all.11.packed_ref), custom_call_target="tpu_custom_call" | custom-call | tf_op jit(solution)/shard_map/unpack/pallas_call | solution.py:317

commit v8 on v7

--- a/solution.py
+++ b/solution.py
@@ -302,22 +302,34 @@
     )(vmem(x), hbm(w_first), hbm(w_second), hbm(gate_pairs), *[vmem(other) for other in others])
 
 
-def unpack_kernel(packed_ref, out_ref):
+def unpack_kernel(packed_ref, out_hbm, rows_ref, copied):
     half = packed_ref.shape[1]
     left = left_half(half)
-    for pair in range(out_ref.shape[1] // LANES):
-        even = packed_ref[2 * pair]
-        odd = packed_ref[2 * pair + 1]
-        cols = slice(pair * LANES, (pair + 1) * LANES)
-        out_ref[:half, cols] = decode(jnp.where(left, even, half_turn(odd)))
-        out_ref[half:, cols] = decode(jnp.where(left, half_turn(even), odd))
+    copies = []
+    for second in range(2):
+        here = pl.ds(second * half, half)
+        for pair in range(rows_ref.shape[1] // LANES):
+            even = packed_ref[2 * pair]
+            odd = packed_ref[2 * pair + 1]
+            cols = slice(pair * LANES, (pair + 1) * LANES)
+            if second:
+                rows_ref[here, cols] = decode(jnp.where(left, half_turn(even), odd))
+            else:
+                rows_ref[here, cols] = decode(jnp.where(left, even, half_turn(odd)))
+        copies.append(pltpu.make_async_copy(rows_ref.at[here], out_hbm.at[here], copied.at[second]))
+        copies[second].start()
+    for copy in copies:
+        copy.wait()
 
 
 def unpack(packed, heads_here):
+    out = (2 * packed.shape[1], heads_here * HEAD_DIM)
     return pl.pallas_call(
         unpack_kernel,
         in_specs=[in_vmem],
-        out_shape=jax.ShapeDtypeStruct((2 * packed.shape[1], heads_here * HEAD_DIM), f32),
+        out_specs=in_hbm,
+        out_shape=jax.ShapeDtypeStruct(out, f32),
+        scratch_shapes=[pltpu.VMEM(out, f32), pltpu.SemaphoreType.DMA((2,))],
         name="unpack",
     )(vmem(packed))
 

time: 55 us -> 55 us (level)
  no operation moved by 1% of the time
where the time goes in v8:
time: 55 us; the launch traced here: 54.7 us
  blocking collectives  40.3 us (73%)
  Pallas kernels  14.4 us (26%)
    all_to_all x1, blocking collectives, on_device(): lax.all_to_all(x, ('seg', 'head'), 0, 0, tiled=True, axis_index_groups=both)  27.7 us
    all_to_all x1, blocking collectives, on_device(): out = lax.all_to_all(out, 'seg', 0, 0, tiled=True, axis_index_groups=lines)  12.6 us
    pallas_call x1, Pallas kernels, work_on_head(): pl.pallas_call(functools.partial(head_kernel, totals_only=totals_only, ac...  12.2 us
    pallas_call x1, Pallas kernels, pack(): pl.pallas_call(functools.partial(pack_kernel, heads_here=heads_here, side...  1.33 us

profile of v8, /device:TPU:0, one launch (start us, length us, event | category | flops | bytes accessed | tf_op | source)
XLA Modules:
  0.0 54.7 jit_solution(6192711268763167449)
XLA Ops:
  0.0 1.3 %pack.1 = bf16[32,96,128]{2,1,0:T(8,128)(2,1)S(1)} custom-call(bf16[64,1536]{1,0:T(8,128)(2,1)} %q_ref.1, bf16[64,1536]{1,0:T(8,128)(2,1)} %k_ref.1, bf16[64,1536]{1,0:T(8,128)(2,1)} %v_ref.1), custom_call_target="tpu_custom_call" | custom-call | tf_op jit(solution)/shard_map/pack/pallas_call | solution.py:109
  1.3 27.7 %all_to_all.10.x_ref = bf16[32,96,128]{2,1,0:T(8,128)(2,1)S(1)} all-to-all(bf16[32,96,128]{2,1,0:T(8,128)(2,1)S(1)} %pack.1), channel_id=1, replica_groups={{0,1,2,3,4,5,6,7,8,9,10,11,12,13,14,15,16,17,18,19,20,21,22,23,24,25,26..., dimensions={0} | all-to-all | bytes 1572864 | tf_op jit(solution)/shard_map/all_to_all | solution.py:346
  29.1 12.2 %head.1 = bf16[8,128,128]{2,1,0:T(8,128)(2,1)S(1)} custom-call(bf16[32,96,128]{2,1,0:T(8,128)(2,1)S(1)} %all_to_all.10.x_ref, f32[6,64,256]{2,1,0:T(8,128)} %first_hbm.1, f32[6,64,256]{2,1,0:T(8,128)} %bitcast.1, f32[2,384]{1,0:T(2,128)} %gate_hbm.1), custom_call_target="tpu_custom_call" | custom-call | tf_op jit(solution)/shard_map/head/pallas_call | solution.py:280
  41.3 12.6 %all_to_all.11.packed_ref = bf16[8,128,128]{2,1,0:T(8,128)(2,1)S(1)} all-to-all(bf16[8,128,128]{2,1,0:T(8,128)(2,1)S(1)} %head.1), channel_id=1, replica_groups={{0,4,8,12,16,20,24,28},{1,5,9,13,17,21,25,29},{2,6,10,14,18,22,26,30},{..., dimensions={0} | all-to-all | bytes 524288 | tf_op jit(solution)/shard_map/all_to_all | solution.py:358
  53.8 0.9 %unpack.1 = f32[256,384]{1,0:T(8,128)} custom-call(bf16[8,128,128]{2,1,0:T(8,128)(2,1)S(1)} %all_to_all.11.packed_ref), custom_call_target="tpu_custom_call" | custom-call | tf_op jit(solution)/shard_map/unpack/pallas_call | solution.py:327

commit v9 on v8

--- a/solution.py
+++ b/solution.py
@@ -244,30 +244,32 @@
                 starts[way][i] = starts[way][i] - inner_rate * other[i]
     gates = gate_ref[:, :dim]
 
-    def enter_model(b, way):
-        w, v = starts[way]
-        if way == 0:
-            w, v = (w - inner_rate * sum_first_ref[b], v - inner_rate * sum_second_ref[b])
-        elif b > 0:
-            w, v = (w + inner_rate * sum_first_ref[b - 1], v + inner_rate * sum_second_ref[b - 1])
-        z = dot(queries(b), jnp.concatenate(split(w), axis=0), NN)
-        return split(gelu(z)), split(centred(v))
-
-    def leave_model(way, entered):
-        u = project(*entered)
-        return gates[way : way + 1] * (u * norm_scale(u))
-
-    ahead, behind = (enter_model(0, 0), enter_model(0, 1))
+    def enter_models(b):
+        (w0, v0), (w1, v1) = starts
+        w0, v0 = (w0 - inner_rate * sum_first_ref[b], v0 - inner_rate * sum_second_ref[b])
+        if b > 0:
+            w1, v1 = (w1 + inner_rate * sum_first_ref[b - 1], v1 + inner_rate * sum_second_ref[b - 1])
+        pairs = [jnp.concatenate(split(w), axis=0) for w in (w0, w1)]
+        z = dot(queries(b), jnp.concatenate(pairs, axis=1), NN)
+        return split(gelu(z)), [split(centred(v)) for v in (v0, v1)]
+
+    def leave_models(entered):
+        (high, low), seconds = entered
+        total = 0.0
+        for way in range(2):
+            cols = slice(way * inner, (way + 1) * inner)
+            u = project((high[:, cols], low[:, cols]), seconds[way])
+            total = total + gates[way : way + 1] * (u * norm_scale(u))
+        return total
+
+    entered = enter_models(0)
     for b in range(batches):
-        last = b + 1 == batches
-        next_ahead = None if last else enter_model(b + 1, 0)
-        result = leave_model(0, ahead)
-        next_behind = None if last else enter_model(b + 1, 1)
-        result = result + leave_model(1, behind)
+        next_entered = None if b + 1 == batches else enter_models(b + 1)
         q = queries(b)[:, :dim].astype(f32)
+        result = leave_models(entered)
         result = encode(attended_ref[here(b), :] + (gates[0:1] + gates[1:2]) * q + result)
         out_ref[b] = jnp.concatenate([result[: part // 2], result[part // 2 :]], axis=1)
-        ahead, behind = (next_ahead, next_behind)
+        entered = next_entered
 
 
 def work_on_head(x, w_first, w_second, gate_pairs, others=(), totals_only=False):

time: 55 us -> 54.8 us (level)
  no operation moved by 1% of the time
where the time goes in v9:
time: 54.8 us; the launch traced here: 54.6 us
  blocking collectives  40.3 us (74%)
  Pallas kernels  14.3 us (26%)
    all_to_all x1, blocking collectives, on_device(): lax.all_to_all(x, ('seg', 'head'), 0, 0, tiled=True, axis_index_groups=both)  27.7 us
    all_to_all x1, blocking collectives, on_device(): out = lax.all_to_all(out, 'seg', 0, 0, tiled=True, axis_index_groups=lines)  12.6 us
    pallas_call x1, Pallas kernels, work_on_head(): pl.pallas_call(functools.partial(head_kernel, totals_only=totals_only, ac...  12 us
    pallas_call x1, Pallas kernels, pack(): pl.pallas_call(functools.partial(pack_kernel, heads_here=heads_here, side...  1.33 us

profile of v9, /device:TPU:0, one launch (start us, length us, event | category | flops | bytes accessed | tf_op | source)
XLA Modules:
  0.0 54.6 jit_solution(3673349553097633932)
XLA Ops:
  0.0 1.3 %pack.1 = bf16[32,96,128]{2,1,0:T(8,128)(2,1)S(1)} custom-call(bf16[64,1536]{1,0:T(8,128)(2,1)} %q_ref.1, bf16[64,1536]{1,0:T(8,128)(2,1)} %k_ref.1, bf16[64,1536]{1,0:T(8,128)(2,1)} %v_ref.1), custom_call_target="tpu_custom_call" | custom-call | tf_op jit(solution)/shard_map/pack/pallas_call | solution.py:109
  1.3 27.7 %all_to_all.10.x_ref = bf16[32,96,128]{2,1,0:T(8,128)(2,1)S(1)} all-to-all(bf16[32,96,128]{2,1,0:T(8,128)(2,1)S(1)} %pack.1), channel_id=1, replica_groups={{0,1,2,3,4,5,6,7,8,9,10,11,12,13,14,15,16,17,18,19,20,21,22,23,24,25,26..., dimensions={0} | all-to-all | bytes 1572864 | tf_op jit(solution)/shard_map/all_to_all | solution.py:348
  29.1 12.0 %head.1 = bf16[8,128,128]{2,1,0:T(8,128)(2,1)S(1)} custom-call(bf16[32,96,128]{2,1,0:T(8,128)(2,1)S(1)} %all_to_all.10.x_ref, f32[6,64,256]{2,1,0:T(8,128)} %first_hbm.1, f32[6,64,256]{2,1,0:T(8,128)} %bitcast.1, f32[2,384]{1,0:T(2,128)} %gate_hbm.1), custom_call_target="tpu_custom_call" | custom-call | tf_op jit(solution)/shard_map/head/pallas_call | solution.py:282
  41.1 12.6 %all_to_all.11.packed_ref = bf16[8,128,128]{2,1,0:T(8,128)(2,1)S(1)} all-to-all(bf16[8,128,128]{2,1,0:T(8,128)(2,1)S(1)} %head.1), channel_id=1, replica_groups={{0,4,8,12,16,20,24,28},{1,5,9,13,17,21,25,29},{2,6,10,14,18,22,26,30},{..., dimensions={0} | all-to-all | bytes 524288 | tf_op jit(solution)/shard_map/all_to_all | solution.py:360
  53.7 0.9 %unpack.1 = f32[256,384]{1,0:T(8,128)} custom-call(bf16[8,128,128]{2,1,0:T(8,128)(2,1)S(1)} %all_to_all.11.packed_ref), custom_call_target="tpu_custom_call" | custom-call | tf_op jit(solution)/shard_map/unpack/pallas_call | solution.py:329
